TPU v7x, 128 devices: a whole 4x4x4 slice. The times are simulated.
128 devices in a mesh: seq: 16 (over y_lo, z, core), mp: 8 (over y_hi, x).
Axes of the slice: x: 4, y: 4 (y_hi: 2, y_lo: 2; y = y_hi * 2 + y_lo), z: 4, core: 2. Of those that a mesh axis runs over, the one named last changes fastest.
Arguments:
- nucleotide_codes: int32 [1048576], P('seq'), may hold values from 0 to 3, as said below
- segment_encoder_map: bfloat16 [512, 1536], P(None, 'mp'), may hold values from -0.5 to 0.5
- mixing_norm_scale: bfloat16 [1536], replicated, may hold values from 0.099609375 to 1.8984375
- asker_probe_content_map: bfloat16 [1536, 3584], P(None, 'mp'), may hold values from -0.15309311 to 0.15309311
- logit_sharpness: float32 [8], P('mp'), may hold values from 3 to 30
- mixing_exit_map: bfloat16 [1536, 1536], P('mp'), may hold values from -0.15625 to 0.15625
- perceptron_norm_scale: bfloat16 [1536], replicated, may hold values from 0.099609375 to 1.8984375
- perceptron_widening_map: bfloat16 [1536, 3072], P(None, 'mp'), may hold values from -0.15625 to 0.15625
- perceptron_narrowing_map: bfloat16 [3072, 1536], P('mp'), may hold values from -0.109375 to 0.109375
- widening_kernel: bfloat16 [5, 1536, 768], P(None, None, 'mp'), may hold values from -0.0625 to 0.0625
Outputs:
- decoded: bfloat16 [768, 16384], P('mp', 'seq')
Inputs may be any that keep to these rules, and one draw needn't show every extreme that they name: `nucleotide_codes`: codes of the bases A, C, G, T; the mix of bases differs from region to region of the sequence.
All inputs are finite; a program needn't handle non-finite values.
Results may differ from a plain program's by a relative error of at most 0.011.
Values may be sent and summed in bfloat16 or wider, within the bound.
A program may use at most 64 MiB of HBM per device.

v0:
```python
import math

import jax
import jax.numpy as jnp
from jax import lax
from jax.sharding import PartitionSpec as P

PROBE_DIM = 128
VALUE = 192
PATCH = 128
WIDTH = 5


epsilon = 1e-06


def extended(cells, sides, width):
    for axis, dim in sides:
        count = lax.axis_size(axis)
        ends = count - 1
        head = lax.slice_in_dim(cells, 0, width, axis=dim)
        tail = lax.slice_in_dim(cells, cells.shape[dim] - width, cells.shape[dim], axis=dim)
        cells = jnp.concatenate(
            [
                lax.ppermute(tail, axis, [(i, (i + 1) % count) for i in range(ends)]),
                cells,
                lax.ppermute(head, axis, [((i + 1) % count, i) for i in range(ends)]),
            ],
            axis=dim,
        )
    return cells


def contract(weight, data):
    return lax.dot_general(
        weight, data, (((0,), (0,)), ((), ())), preferred_element_type=jnp.float32
    )


def fold_channels(local, combine, start_value):
    return combine(start_value, lax.all_gather(local, "mp", axis=0, tiled=True), jnp.int32(0))


def normed_product(local, gain, weight):
    width_all = gain.shape[0]
    entry_tally = local.shape[1]

    def combine(carry, piece, start):
        wide = piece.astype(jnp.float32)
        part_gain = gain.astype(jnp.float32)
        scaled = (wide * part_gain[:, None]).astype(jnp.bfloat16)
        total = contract(weight, scaled)
        squares = jnp.sum(wide * wide, axis=0)
        return (total, squares)

    start_value = (
        jnp.zeros((weight.shape[1], entry_tally), jnp.float32),
        jnp.zeros((entry_tally,), jnp.float32),
    )
    total, squares = fold_channels(local, combine, start_value)
    return total * lax.rsqrt(squares / width_all + epsilon)[None, :]


def cosine_mixing_layer(affine_transform, logit_sharpness, entry_tally):
    lens_collection = logit_sharpness.shape[0]
    shaped = affine_transform.reshape(lens_collection, 2 * PROBE_DIM + VALUE, entry_tally)
    asker_vectors = shaped[:, :PROBE_DIM]
    probe_vectors = shaped[:, PROBE_DIM : 2 * PROBE_DIM]
    asker_vectors = (
        asker_vectors
        * lax.rsqrt(jnp.mean(asker_vectors * asker_vectors, axis=1, keepdims=True) + epsilon)
    ).astype(jnp.bfloat16)
    probe_vectors = (
        probe_vectors
        * lax.rsqrt(jnp.mean(probe_vectors * probe_vectors, axis=1, keepdims=True) + epsilon)
    ).astype(jnp.bfloat16)
    content_vectors = shaped[:, 2 * PROBE_DIM :].astype(jnp.bfloat16)
    packed = jnp.concatenate([probe_vectors, content_vectors], axis=1).reshape(
        lens_collection * (PROBE_DIM + VALUE), entry_tally
    )
    resolution_ratio = logit_sharpness / PROBE_DIM

    def combine(carry, piece, start):
        length = piece.shape[1]
        block = math.gcd(length, 512)
        shaped_piece = piece.reshape(lens_collection, PROBE_DIM + VALUE, length)

        def step(index, inner):
            numer, denom = inner
            part = lax.dynamic_slice_in_dim(shaped_piece, index * block, block, 2)
            scores = (
                jnp.einsum(
                    "hdq,hdk->hqk",
                    asker_vectors,
                    part[:, :PROBE_DIM],
                    preferred_element_type=jnp.float32,
                )
                * resolution_ratio[:, None, None]
            )
            weights = jnp.exp(scores)
            denom = denom + jnp.sum(weights, axis=2)
            numer = numer + jnp.einsum(
                "hqk,hdk->hdq",
                weights.astype(jnp.bfloat16),
                part[:, PROBE_DIM:],
                preferred_element_type=jnp.float32,
            )
            return (numer, denom)

        return lax.fori_loop(0, length // block, step, carry)

    start_value = (
        jnp.zeros((lens_collection, VALUE, entry_tally), jnp.float32),
        jnp.zeros((lens_collection, entry_tally), jnp.float32),
    )
    numer, denom = combine(
        start_value, lax.all_gather(packed, "seq", axis=1, tiled=True), jnp.int32(0)
    )
    return (
        (numer / denom[:, None, :])
        .astype(jnp.bfloat16)
        .reshape(lens_collection * VALUE, entry_tally)
    )


def channel_sums(weight, inner):
    return lax.psum_scatter(contract(weight, inner), "mp", scatter_dimension=0, tiled=True)


def decode(stream, weight):
    entry_tally = stream.shape[1]
    outs = weight.shape[2]
    doubled = jnp.repeat(stream, 2, axis=1)
    padded = extended(doubled, (("seq", 1),), 2)

    def combine(total, piece, start):
        for shift in range(WIDTH):
            total = total + contract(weight[shift], piece[:, shift : shift + 2 * entry_tally])
        return total

    start_value = jnp.zeros((outs, 2 * entry_tally), jnp.float32)
    total = fold_channels(padded, combine, start_value)
    return total.astype(jnp.bfloat16)


def per_device(
    nucleotide_codes,
    segment_encoder_map,
    mixing_norm_scale,
    asker_probe_content_map,
    logit_sharpness,
    mixing_exit_map,
    perceptron_norm_scale,
    perceptron_widening_map,
    perceptron_narrowing_map,
    widening_kernel,
):
    entry_tally = nucleotide_codes.shape[0] // PATCH
    codes = nucleotide_codes.reshape(entry_tally, PATCH)
    onehot = (
        (codes[:, :, None] == jnp.arange(4, dtype=jnp.int32))
        .astype(jnp.bfloat16)
        .reshape(entry_tally, PATCH * 4)
    )
    stream = lax.dot_general(
        segment_encoder_map, onehot, (((0,), (1,)), ((), ())), preferred_element_type=jnp.float32
    ).astype(jnp.bfloat16)
    affine_transform = normed_product(stream, mixing_norm_scale, asker_probe_content_map)
    mixing_result = cosine_mixing_layer(affine_transform, logit_sharpness, entry_tally)
    mixed = (stream.astype(jnp.float32) + channel_sums(mixing_exit_map, mixing_result)).astype(
        jnp.bfloat16
    )
    inner = jnp.maximum(
        normed_product(mixed, perceptron_norm_scale, perceptron_widening_map), 0.0
    ).astype(jnp.bfloat16)
    final = (mixed.astype(jnp.float32) + channel_sums(perceptron_narrowing_map, inner)).astype(
        jnp.bfloat16
    )
    return decode(final, widening_kernel)


def solution(mesh):
    in_specs = (
        P("seq"),
        P(None, "mp"),
        P(),
        P(None, "mp"),
        P("mp"),
        P("mp", None),
        P(),
        P(None, "mp"),
        P("mp", None),
        P(None, None, "mp"),
    )
    out_specs = P("mp", "seq")
    return jax.shard_map(
        per_device, mesh=mesh, in_specs=in_specs, out_specs=out_specs, check_vma=False
    )
```

profile of v0, /device:TPU:1, one launch (start us, length us, event | category | flops | bytes accessed | tf_op | source)
XLA Modules:
  0.0 466.1 jit_solution(1005854938022642429)
XLA Ops:
  8.4 2.0 fusion.62
  10.5 52.9 %all-gather.6.cloned.1.call-done = bf16[1536,512]{1,0:T(8,128)(2,1)} async-done(((bf16[192,512]{1,0:T(8,128)(2,1)}), bf16[1536,512]{1,0:T(8,128)(2,1)}) %all-gather.6.cloned.1.call-update) | async-done | bytes 1572880 | tf_op jit(solution)/shard_map/all_gather | solution.py:41
  63.4 1.8 fusion.8
  65.2 2.4 fusion.30
  69.3 39.7 %all-gather.12.cloned.1.call-done = bf16[1,320,8192]{2,1,0:T(8,128)(2,1)} async-done(((bf16[1,320,512]{2,1,0:T(8,128)(2,1)}), bf16[1,320,8192]{2,1,0:T(8,128)(2,1)}) %all-gather.12.cloned.1.call-update) | async-done | bytes 5242896 | tf_op jit(solution)/shard_map/all_gather | solution.py:117
  109.0 40.7 %while.16 = (s32[]{:T(128)}, f32[1,192,512]{2,1,0:T(8,128)S(1)}, f32[1,512]{1,0:T(1,128)S(1)}, bf16[1,320,8192]{2,1,0:T(8,128)(2,1)}, bf16[1,128,512]{2,1,0:T(8,...) while((s32[]{:T(128)}, f32[1,192,512]{2,1,0:T(8,128)S(1)}, ...), condition=%wide.region_5.0_spmd.clone, body=%wide.region_3.0_spmd.clone.sunk | while | flops 168755712 | bytes 2302654 | solution.py:110
  109.0 1.3 fusion.92
  110.3 1.2 fusion.93
  111.6 1.3 fusion.92
  112.9 1.2 fusion.93
  114.1 1.3 fusion.92
  115.4 1.2 fusion.93
  116.7 1.3 fusion.92
  117.9 1.2 fusion.93
  119.2 1.3 fusion.92
  120.5 1.2 fusion.93
  121.8 1.3 fusion.92
  123.0 1.2 fusion.93
  124.3 1.3 fusion.92
  125.6 1.2 fusion.93
  126.9 1.3 fusion.92
  128.1 1.2 fusion.93
  129.4 1.3 fusion.92
  130.7 1.2 fusion.93
  131.9 1.3 fusion.92
  133.2 1.2 fusion.93
  134.5 1.3 fusion.92
  137.0 1.3 fusion.92
  139.6 1.3 fusion.92
  142.1 1.3 fusion.92
  144.7 1.3 fusion.92
  145.9 1.2 fusion.93
  147.2 1.3 fusion.92
  148.5 1.2 fusion.93
  149.8 2.3 convolution_bitcast_fusion.2
  152.1 78.6 %reduce-scatter.3.cloned.1.call-done = f32[192,512]{1,0:T(8,128)} async-done(((f32[1536,512]{1,0:T(8,128)}), f32[192,512]{1,0:T(8,128)}) %reduce-scatter.3.cloned.1.call-update) | async-done | bytes 393232 | tf_op jit(solution)/shard_map/reduce_scatter | solution.py:127
  230.7 1.7 add_convert_fusion.1
  232.5 50.5 %all-gather.8.cloned.1.call-done = bf16[1536,512]{1,0:T(8,128)(2,1)} async-done(((bf16[192,512]{1,0:T(8,128)(2,1)}), bf16[1536,512]{1,0:T(8,128)(2,1)}) %all-gather.8.cloned.1.call-update) | async-done | bytes 1572880 | tf_op jit(solution)/shard_map/all_gather | solution.py:41
  283.0 1.8 fusion.10
  284.8 5.8 %convolution_bitcast_fusion.1 = f32[1536,512]{1,0:T(8,128)} fusion(bf16[384,1536]{1,0:T(8,128)(2,1)} %param.20, bf16[1536,384]{1,0:T(8,128)(2,1)} %param.19, bf16[1536,512]{1,0:T(8,128)(2,1)} %all-gather.8.cloned.1.call-done, f32[1536]{0:T(1024)S(1)} %convert_element_type.73, f32[512]{0:T(512)S(1)} %add_rsqrt_fusion), kind=kOutput, calls=%fused_computation.16 | convolution fusion | flops 1210908672 | bytes 7086080 | tf_op jit(solution)/shard_map/dot_general | solution.py:35
  290.6 79.3 %reduce-scatter.5.cloned.1.call-done = f32[192,512]{1,0:T(8,128)} async-done(((f32[1536,512]{1,0:T(8,128)}), f32[192,512]{1,0:T(8,128)}) %reduce-scatter.5.cloned.1.call-update) | async-done | bytes 393232 | tf_op jit(solution)/shard_map/reduce_scatter | solution.py:127
  372.0 5.1 %collective-permute-start = (bf16[192,2]{0,1:T(2,128)(2,1)S(1)}, bf16[192,2]{0,1:T(2,128)(2,1)S(1)}, u32[]{:S(2)}, u32[]{:S(2)}) collective-permute-start(bf16[192,2]{0,1:T(2,128)(2,1)S(1)} %get-tuple-element.157), channel_id=1, source_target_pairs={{0,8},{8,16},{16,24},{24,32},{32,40},{40,48},{48,56},{56,64},{64,7... | collective-permute-start | bytes 2312 | tf_op jit(solution)/shard_map/ppermute | solution.py:25
  377.1 2.1 collective-permute-start.1
  379.2 2.8 collective-permute-done.1
  384.0 65.9 %all-gather.10.cloned.1.call-done = bf16[1536,1028]{1,0:T(8,128)(2,1)} async-done(((bf16[192,1028]{1,0:T(8,128)(2,1)}), bf16[1536,1028]{1,0:T(8,128)(2,1)}) %all-gather.10.cloned.1.call-update) | async-done | bytes 3158032 | tf_op jit(solution)/shard_map/all_gather | solution.py:41
  449.9 3.3 fusion.11
  453.3 2.2 fusion.13
  457.9 1.3 fusion.59
  (74 shorter events, 14.5 us)
Async XLA Ops:
  6.5 58.7 %copy-start = (bf16[1536,448]{0,1:T(8,128)(2,1)S(1)}, bf16[1536,448]{0,1:T(8,128)(2,1)}, u32[]{:S(2)}) copy-start(bf16[1536,448]{0,1:T(8,128)(2,1)} %param.15) | copy-start | bytes 4128772
  6.5 4.0 copy-start.6
  6.5 56.9 %all-gather.6.cloned.1.call-start = ((), (), s32[]{:S(2)}) async-start(), calls=%async_computation.2 | async-start | bytes 1769472 | tf_op jit(solution)/shard_map/all_gather | solution.py:41
  10.5 98.5 %all-gather.12.cloned.1.call-start = ((), (), s32[]{:S(2)}) async-start(), calls=%async_computation.7 | async-start | bytes 5570560 | tf_op jit(solution)/shard_map/all_gather | solution.py:117
  68.6 162.1 %reduce-scatter.3.cloned.1.call-start = ((), (), s32[]{:S(2)}) async-start(), calls=%async_computation.3 | async-start | bytes 3538944 | tf_op jit(solution)/shard_map/reduce_scatter | solution.py:127
  109.0 40.7 %copy-start.4 = (bf16[192,1536]{1,0:T(8,128)(2,1)S(1)}, bf16[192,1536]{1,0:T(8,128)(2,1)}, u32[]{:S(2)}) copy-start(bf16[192,1536]{1,0:T(8,128)(2,1)} %param.17) | copy-start | bytes 1769476
  149.7 81.0 %copy-start.3 = (bf16[192,512]{1,0:T(8,128)(2,1)S(1)}, bf16[192,512]{1,0:T(8,128)(2,1)}, u32[]{:S(2)}) copy-start(bf16[192,512]{1,0:T(8,128)(2,1)} %fusion.62) | copy-start | bytes 589828
  149.8 82.8 %copy-start.7 = (bf16[1536]{0:T(1024)(128)(2,1)S(1)}, bf16[1536]{0:T(1024)(128)(2,1)}, u32[]{:S(2)}) copy-start(bf16[1536]{0:T(1024)(128)(2,1)} %param.18) | copy-start | bytes 9220
  152.1 130.9 %all-gather.8.cloned.1.call-start = ((), (), s32[]{:S(2)}) async-start(), calls=%async_computation.4 | async-start | bytes 1769472 | tf_op jit(solution)/shard_map/all_gather | solution.py:41
  232.5 137.5 %reduce-scatter.5.cloned.1.call-start = ((), (), s32[]{:S(2)}) async-start(), calls=%async_computation.5 | async-start | bytes 3538944 | tf_op jit(solution)/shard_map/reduce_scatter | solution.py:127
  290.6 79.4 %copy-start.2 = (bf16[192,512]{1,0:T(8,128)(2,1)S(1)}, bf16[192,512]{1,0:T(8,128)(2,1)}, u32[]{:S(2)}) copy-start(bf16[192,512]{1,0:T(8,128)(2,1)} %add_convert_fusion.1) | copy-start | bytes 589828
  290.6 159.3 %all-gather.10.cloned.1.call-start = ((), (), s32[]{:S(2)}) async-start(), calls=%async_computation.6 | async-start | bytes 3981312 | tf_op jit(solution)/shard_map/all_gather | solution.py:41
  372.0 7.3 %collective-permute-start = (bf16[192,2]{0,1:T(2,128)(2,1)S(1)}, bf16[192,2]{0,1:T(2,128)(2,1)S(1)}, u32[]{:S(2)}, u32[]{:S(2)}) collective-permute-start(bf16[192,2]{0,1:T(2,128)(2,1)S(1)} %get-tuple-element.157), channel_id=1, source_target_pairs={{0,8},{8,16},{16,24},{24,32},{32,40},{40,48},{48,56},{56,64},{64,7... | collective-permute-start | bytes 2312 | tf_op jit(solution)/shard_map/ppermute | solution.py:25
  377.1 4.9 %collective-permute-start.1 = (bf16[192,2]{0,1:T(2,128)(2,1)S(1)}, bf16[192,2]{0,1:T(2,128)(2,1)S(1)}, u32[]{:S(2)}, u32[]{:S(2)}) collective-permute-start(bf16[192,2]{0,1:T(2,128)(2,1)S(1)} %get-tuple-element.156), channel_id=1, source_target_pairs={{8,0},{16,8},{24,16},{32,24},{40,32},{48,40},{56,48},{64,56},{72,6... | collective-permute-start | bytes 2312 | tf_op jit(solution)/shard_map/ppermute | solution.py:27
  449.9 3.4 copy-start.1
  453.3 2.3 copy-start.5
Sparse Core Ops, SparseCore 0:
  10.6 52.8 all-gather.5
  68.7 40.2 all-gather.11
  152.2 78.4 reduce-scatter.2
  233.1 49.7 all-gather.7
  290.7 79.2 reduce-scatter.4
  384.1 65.7 all-gather.9
where the time goes:
time: 467 us; the launch traced here: 466 us
  waiting for transfers between devices  370 us (79%)
  matrix products  61.6 us (13%)
  between operations  14.4 us (3%)
  other arithmetic  7.49 us (2%)
  starting transfers between devices  7.45 us (2%)
  local copies, waits for them, and re-layouts  4.82 us (1%)
    all_gather x3, waiting for transfers between devices, fold_channels(): lax.all_gather(local, 'mp', axis=0, tiled=True)  169 us
    reduce_scatter x2, waiting for transfers between devices, channel_sums(): lax.psum_scatter(contract(weight, inner), 'mp', scatter_dimension=0, tile...  158 us
    all_gather x1, waiting for transfers between devices, cosine_mixing_layer(): lax.all_gather(packed, 'seq', axis=1, tiled=True)  39.7 us
    dot_general x16, matrix products, step(): jnp.einsum('hdq,hdk->hqk', asker_vectors, part[:, :PROBE_DIM], preferred_...  20.2 us
    dot_general x8, matrix products, contract(): lax.dot_general(weight, data, (((0,), (0,)), ((), ())), preferred_element...  19.7 us
    dot_general x16, matrix products, step(): jnp.einsum('hqk,hdk->hdq', weights.astype(jnp.bfloat16), part[:, PROBE_DI...  19.7 us
  transfers between devices with their start and end apart: 8, of which 7 were waited for; matrix products, arithmetic and copies ran while one was open for 0% of the time, Pallas kernels for 0%

commit v1 on v0

v1 whole, which is shorter than its diff:
```python
import functools

import jax
import jax.numpy as jnp
from jax import lax
from jax.experimental import pallas as pl
from jax.experimental.pallas import tpu as pltpu
from jax.sharding import PartitionSpec as P

MESH = pl.DeviceIdType.MESH
BF = jnp.bfloat16
F32 = jnp.float32

D = 1536
T = 512
PROBE = 128
VALUE = 192
HIDDEN = 384
OUTS = 96
PATCH = 128
EPS = 1e-06
LOG2E = 1.4426950408889634


def dot(a, b):
    return jnp.dot(a, b, preferred_element_type=F32)


def dot_nt(a, b):
    return lax.dot_general(a, b, (((1,), (1,)), ((), ())), preferred_element_type=F32)


def dot_tn(a, b):
    return lax.dot_general(a, b, (((0,), (0,)), ((), ())), preferred_element_type=F32)


def one_hot_codes(codes):
    wide = codes.astype(F32)
    parts = [jnp.where(wide == float(b), 1.0, 0.0).astype(BF) for b in range(4)]
    return jnp.concatenate(parts, axis=1)


def gain_columns(row, width):
    spread = jnp.broadcast_to(row, (16, D)).astype(BF)
    return dot_tn(spread, jnp.full((16, width), 1.0 / 16.0, BF))


def token_columns(row, width):
    high = row.astype(BF)
    low = (row - high.astype(F32)).astype(BF)
    both = jnp.concatenate(
        [jnp.broadcast_to(high, (16, T)), jnp.broadcast_to(low, (16, T))], axis=0
    )
    return dot_tn(both, jnp.full((32, width), 1.0 / 16.0, BF))


def kernel(
    codes_hbm,
    e_hbm,
    g1_ref,
    w_hbm,
    sharp_ref,
    exit_hbm,
    g2_ref,
    widen_hbm,
    narrow_hbm,
    conv_hbm,
    out_ref,
    codes_i,
    codes_all,
    codes_sib,
    e_loc,
    et_full,
    w_loc,
    wg_t,
    m_t,
    exit_full,
    exit_t,
    stream_t,
    u_all,
    u_sib,
    keys,
    vals,
    queries,
    acc,
    part_recv,
    att_full,
    mixed_t,
    widen_loc,
    widen_t,
    narrow_loc,
    narrow_t,
    inner_t,
    rs_send,
    rs_recv,
    fin_full,
    conv_loc,
    conv_t,
    taps,
    edge_send,
    edge_recv,
    in_sem,
    codes_ss,
    codes_rs,
    e_ss,
    e_rs,
    ef_ss,
    ef_rs,
    x_ss,
    x_rs,
    xf_ss,
    xf_rs,
    u_ss,
    u_rs,
    p_ss,
    p_rs,
    att_ss,
    att_rs,
    sum_ss,
    sum_rs,
    fin_ss,
    fin_rs,
    edge_ss,
    edge_rs,
):
    s = lax.axis_index("seq")
    m = lax.axis_index("mp")
    core = s % 2
    j = s // 2
    sib = s + 1 - 2 * core
    far = (s + 15 + 2 * core) % 16
    hi = m // 4

    def weight_peer(d):
        m2 = (m + d) % 8
        return ((s + 8 * ((m2 // 4 + hi) % 2)) % 16, m2)

    def seq_peer(d):
        return (2 * ((j + d) % 8) + core, m)

    def mp_peer(d):
        return (s, (m + d) % 8)

    def send(src, dst, ss, rs, dev):
        copy = pltpu.make_async_remote_copy(
            src_ref=src, dst_ref=dst, send_sem=ss, recv_sem=rs, device_id=dev, device_id_type=MESH
        )
        return copy

    pending = []

    def push(src, dst, ss, rs, dev):
        copy = send(src, dst, ss, rs, dev)
        copy.start()
        pending.append(copy)

    def arrive(dst, ss, rs):
        send(dst, dst, ss, rs, (sib, m)).wait_recv()

    local = [
        pltpu.make_async_copy(codes_hbm, codes_i, in_sem.at[0]),
        pltpu.make_async_copy(e_hbm, e_loc, in_sem.at[1]),
        pltpu.make_async_copy(w_hbm, w_loc, in_sem.at[2]),
        pltpu.make_async_copy(
            exit_hbm, exit_full.at[pl.ds(pl.multiple_of(m * 192, 192), 192)], in_sem.at[3]
        ),
        pltpu.make_async_copy(widen_hbm, widen_loc, in_sem.at[4]),
        pltpu.make_async_copy(narrow_hbm, narrow_loc, in_sem.at[5]),
        pltpu.make_async_copy(conv_hbm, conv_loc, in_sem.at[6]),
    ]
    for copy in local:
        copy.start()

    barrier = pltpu.get_barrier_semaphore()
    greet = [(s, (m + d) % 8) for d in range(1, 8)]
    greet += [((s + 8) % 16, (1 - hi) * 4 + x) for x in range(4)]
    greet += [seq_peer(d) for d in range(1, 8)]
    greet += [(sib, m), (far, m)]
    for dev in greet:
        pl.semaphore_signal(barrier, inc=1, device_id=dev, device_id_type=MESH)

    local[0].wait()
    codes_all[j] = codes_i[...].astype(BF)
    local[1].wait()
    rows = lax.broadcasted_iota(jnp.int32, (T, T), 0)
    cols = lax.broadcasted_iota(jnp.int32, (T, T), 1)
    order = jnp.where(rows == 4 * (cols % PATCH) + cols // PATCH, 1.0, 0.0).astype(BF)
    et_full[pl.ds(pl.multiple_of(m * 192, 192), 192), :] = dot_tn(e_loc[...], order).astype(BF)

    pl.semaphore_wait(barrier, len(greet))

    def half(ref, shard, c):
        return ref.at[pl.ds(pl.multiple_of(shard * 192 + c * 96, 96), 96)]

    for d in range(1, 8):
        mine = half(et_full, m, core)
        push(mine, mine, e_ss.at[d], e_rs.at[d], weight_peer(d))
    push(codes_all.at[j], codes_sib, codes_ss.at[0], codes_rs.at[0], (sib, m))
    for d in range(1, 8):
        push(codes_all.at[j], codes_all.at[j], codes_ss.at[d], codes_rs.at[d], seq_peer(d))
    local[3].wait()
    for d in range(1, 8):
        mine = half(exit_full, m, core)
        push(mine, mine, x_ss.at[d], x_rs.at[d], weight_peer(d))

    local[2].wait()
    gain = gain_columns(g1_ref[...], 128)
    scaled_w = (
        w_loc[...].astype(F32) * jnp.concatenate([gain] * 3 + [gain[:, :64]], axis=1)
    ).astype(BF)
    wg_t[0:448, :] = scaled_w.T
    wg_t[448:512, :] = jnp.zeros((64, D), BF)

    for d in range(1, 8):
        shard = (m + 8 - d) % 8
        landed = half(et_full, shard, core)
        arrive(landed, e_ss.at[d], e_rs.at[d])
        push(landed, landed, ef_ss.at[d], ef_rs.at[d], (sib, m))
    for d in range(1, 8):
        landed = half(et_full, (m + 8 - d) % 8, 1 - core)
        arrive(landed, ef_ss.at[d], ef_rs.at[d])

    mine_hot = one_hot_codes(codes_all[j])

    def stream_step(i, total):
        at = pl.ds(pl.multiple_of(i * 256, 256), 256)
        tile = dot_nt(et_full[at, :], mine_hot).astype(BF)
        stream_t[at, :] = tile
        wide = tile.astype(F32)
        return total + jnp.sum(wide * wide, axis=0, keepdims=True)

    squares = lax.fori_loop(0, D // 256, stream_step, jnp.zeros((1, T), F32))
    u_all[j] = jnp.broadcast_to(squares / D + EPS, (8, T))
    push(u_all.at[j], u_sib, u_ss.at[0], u_rs.at[0], (sib, m))
    for d in range(1, 8):
        push(u_all.at[j], u_all.at[j], u_ss.at[d], u_rs.at[d], seq_peer(d))

    m_t[...] = dot(wg_t[...], et_full[...]).astype(BF)

    lanes = lax.broadcasted_iota(jnp.int32, (T, 256), 1)

    def keys_values(block, at):
        hot = one_hot_codes(codes_all[block])
        raw = dot_nt(hot, m_t[128:512, :])
        spread = token_columns(u_all[block][0:1], 128)
        key = raw[:, :128]
        mean = jnp.mean(key * key, axis=1, keepdims=True)
        keys[at, :] = (key * lax.rsqrt(mean + EPS * spread)).astype(BF)
        inverse = lax.rsqrt(spread)
        value = raw[:, 128:] * jnp.concatenate([inverse, inverse], axis=1)
        vals[at, :] = jnp.where(lanes < VALUE, value, 1.0).astype(BF)

    factor = sharp_ref[0] * (LOG2E / PROBE)

    def make_queries(slot, codes, u_row):
        raw = dot_nt(one_hot_codes(codes), m_t[0:128, :])
        spread = token_columns(u_row, 128)
        mean = jnp.mean(raw * raw, axis=1, keepdims=True)
        queries[slot] = (raw * (lax.rsqrt(mean + EPS * spread) * factor)).astype(BF)

    keys_values(j, pl.ds(0, T))
    make_queries(1, codes_all[j], u_all[j][0:1])
    arrive(codes_sib, codes_ss.at[0], codes_rs.at[0])
    arrive(u_sib, u_ss.at[0], u_rs.at[0])
    make_queries(0, codes_sib[...], u_sib[0:1])
    for d in range(1, 8):
        block = (j + 8 - d) % 8
        arrive(codes_all.at[block], codes_ss.at[d], codes_rs.at[d])
        arrive(u_all.at[block], u_ss.at[d], u_rs.at[d])
        keys_values(block, pl.ds(d * T, T))

    def attend(slot):
        def chunk(q, _):
            at = pl.ds(pl.multiple_of(q * 256, 256), 256)
            asked = queries[slot, at, :]

            def step(k, total):
                span = pl.ds(pl.multiple_of(k * 1024, 1024), 1024)
                weights = jnp.exp2(dot_nt(asked, keys[span, :])).astype(BF)
                return total + dot(weights, vals[span, :])

            acc[slot, at, :] = lax.fori_loop(0, 4, step, jnp.zeros((256, 256), F32), unroll=True)
            return 0

        lax.fori_loop(0, 2, chunk, 0)

    attend(0)
    push(acc.at[0], part_recv, p_ss.at[0], p_rs.at[0], (sib, m))

    for d in range(1, 8):
        landed = half(exit_full, (m + 8 - d) % 8, core)
        arrive(landed, x_ss.at[d], x_rs.at[d])
        push(landed, landed, xf_ss.at[d], xf_rs.at[d], (sib, m))

    attend(1)
    arrive(part_recv, p_ss.at[0], p_rs.at[0])
    whole = acc[1] + part_recv[...]
    attended = whole[:, :VALUE] / whole[:, VALUE : VALUE + 1]
    my_rows = pl.ds(pl.multiple_of(m * 192, 192), 192)
    att_full[my_rows, :] = attended.astype(BF).T
    for d in range(1, 8):
        push(
            att_full.at[my_rows], att_full.at[my_rows], att_ss.at[d], att_rs.at[d], mp_peer(d)
        )

    local[4].wait()
    gain = gain_columns(g2_ref[...], 128)
    widen_t[...] = (
        (widen_loc[...].astype(F32) * jnp.concatenate([gain] * 3, axis=1)).astype(BF).T
    )
    local[5].wait()
    narrow_t[...] = narrow_loc[...].T
    local[6].wait()
    pair = conv_loc[0].astype(F32)
    second = conv_loc[1].astype(F32)
    third = conv_loc[2].astype(F32)
    fourth = conv_loc[3].astype(F32)
    last = conv_loc[4].astype(F32)

    def put_tap(index, even, odd):
        conv_t[index, 0:OUTS, :] = even.astype(BF).T
        conv_t[index, OUTS : 2 * OUTS, :] = odd.astype(BF).T

    put_tap(0, pair + second, pair)
    put_tap(1, third + fourth, second + third)
    put_tap(2, last, fourth + last)

    for d in range(1, 8):
        landed = half(exit_full, (m + 8 - d) % 8, 1 - core)
        arrive(landed, xf_ss.at[d], xf_rs.at[d])

    def turn_exit(i, _):
        at = pl.ds(pl.multiple_of(i * 256, 256), 256)
        exit_t[at, :] = exit_full[:, at].T
        return 0

    lax.fori_loop(0, D // 256, turn_exit, 0)

    for d in range(1, 8):
        landed = att_full.at[pl.ds(pl.multiple_of(((m + 8 - d) % 8) * 192, 192), 192)]
        arrive(landed, att_ss.at[d], att_rs.at[d])

    def exit_step(i, total):
        at = pl.ds(pl.multiple_of(i * 256, 256), 256)
        tile = (stream_t[at, :].astype(F32) + dot(exit_t[at, :], att_full[...])).astype(BF)
        mixed_t[at, :] = tile
        wide = tile.astype(F32)
        return total + jnp.sum(wide * wide, axis=0, keepdims=True)

    squares = lax.fori_loop(0, D // 256, exit_step, jnp.zeros((1, T), F32))
    second_scale = lax.rsqrt(squares / D + EPS)
    inner = dot(widen_t[...], mixed_t[...]) * second_scale
    inner_t[...] = jnp.maximum(inner, 0.0).astype(BF)

    for d in range(1, 8):
        slice_rows = pl.ds(pl.multiple_of(((m + d) % 8) * 192, 192), 192)
        rs_send[d] = dot(narrow_t[slice_rows, :], inner_t[...]).astype(BF)
        push(rs_send.at[d], rs_recv.at[d], sum_ss.at[d], sum_rs.at[d], mp_peer(d))
    total = mixed_t[my_rows, :].astype(F32) + dot(narrow_t[my_rows, :], inner_t[...])
    for d in range(1, 8):
        arrive(rs_recv.at[d], sum_ss.at[d], sum_rs.at[d])
        total = total + rs_recv[d].astype(F32)
    fin_full[my_rows, :] = total.astype(BF)
    for d in range(1, 8):
        push(
            fin_full.at[my_rows], fin_full.at[my_rows], fin_ss.at[d], fin_rs.at[d], mp_peer(d)
        )
    for d in range(1, 8):
        landed = fin_full.at[pl.ds(pl.multiple_of(((m + 8 - d) % 8) * 192, 192), 192)]
        arrive(landed, fin_ss.at[d], fin_rs.at[d])

    edge_send[0] = dot(conv_t[0], fin_full[:, T - 128 :])
    edge_send[1] = dot(conv_t[2], fin_full[:, :128])
    push(edge_send.at[0], edge_recv.at[0], edge_ss.at[0], edge_rs.at[0], ((s + 1) % 16, m))
    push(edge_send.at[1], edge_recv.at[1], edge_ss.at[1], edge_rs.at[1], ((s + 15) % 16, m))
    before = dot(conv_t[0], fin_full[...])
    here = dot(conv_t[1], fin_full[...])
    after = dot(conv_t[2], fin_full[...])
    arrive(edge_recv.at[0], edge_ss.at[0], edge_rs.at[0])
    arrive(edge_recv.at[1], edge_ss.at[1], edge_rs.at[1])
    left = jnp.where(s > 0, edge_recv[0][:, 127:128], 0.0)
    right = jnp.where(s < 15, edge_recv[1][:, 0:1], 0.0)
    before = jnp.concatenate([left, before[:, : T - 1]], axis=1)
    after = jnp.concatenate([after[:, 1:], right], axis=1)
    result = (before + here + after).astype(BF)
    rows = lax.broadcasted_iota(jnp.int32, (256, 256), 0)
    cols = lax.broadcasted_iota(jnp.int32, (256, 256), 1)
    weave = jnp.where(cols == 2 * (rows % 128) + rows // 128, 1.0, 0.0).astype(BF)
    for b in range(4):
        pair = jnp.concatenate(
            [
                result[:OUTS, b * 128 : (b + 1) * 128],
                result[OUTS:, b * 128 : (b + 1) * 128],
            ],
            axis=1,
        )
        out_ref[:, b * 256 : (b + 1) * 256] = dot(pair, weave).astype(BF)

    for copy in pending:
        copy.wait_send()


def per_device(codes, e, g1, w, sharp, exit_map, g2, widen, narrow, conv):
    any_space = pl.BlockSpec(memory_space=pl.ANY)
    vmem = pl.BlockSpec(memory_space=pltpu.VMEM)
    smem = pl.BlockSpec(memory_space=pltpu.SMEM)
    dma = pltpu.SemaphoreType.DMA((8,))
    return pl.pallas_call(
        kernel,
        out_shape=jax.ShapeDtypeStruct((OUTS, 2 * T), BF),
        in_specs=[
            any_space,
            any_space,
            vmem,
            any_space,
            smem,
            any_space,
            vmem,
            any_space,
            any_space,
            any_space,
        ],
        out_specs=vmem,
        scratch_shapes=[
            pltpu.VMEM((T, PATCH), jnp.int32),
            pltpu.VMEM((8, T, PATCH), BF),
            pltpu.VMEM((T, PATCH), BF),
            pltpu.VMEM((T, 192), BF),
            pltpu.VMEM((D, T), BF),
            pltpu.VMEM((D, 448), BF),
            pltpu.VMEM((T, D), BF),
            pltpu.VMEM((T, T), BF),
            pltpu.VMEM((D, D), BF),
            pltpu.VMEM((D, D), BF),
            pltpu.VMEM((D, T), BF),
            pltpu.VMEM((8, 8, T), F32),
            pltpu.VMEM((8, T), F32),
            pltpu.VMEM((8 * T, PROBE), BF),
            pltpu.VMEM((8 * T, 256), BF),
            pltpu.VMEM((2, T, PROBE), BF),
            pltpu.VMEM((2, T, 256), F32),
            pltpu.VMEM((T, 256), F32),
            pltpu.VMEM((D, T), BF),
            pltpu.VMEM((D, T), BF),
            pltpu.VMEM((D, HIDDEN), BF),
            pltpu.VMEM((HIDDEN, D), BF),
            pltpu.VMEM((HIDDEN, D), BF),
            pltpu.VMEM((D, HIDDEN), BF),
            pltpu.VMEM((HIDDEN, T), BF),
            pltpu.VMEM((8, 192, T), BF),
            pltpu.VMEM((8, 192, T), BF),
            pltpu.VMEM((D, T), BF),
            pltpu.VMEM((5, D, OUTS), BF),
            pltpu.VMEM((3, 2 * OUTS, D), BF),
            pltpu.VMEM((2 * OUTS, T), F32),
            pltpu.VMEM((2, 2 * OUTS, 128), F32),
            pltpu.VMEM((2, 2 * OUTS, 128), F32),
        ]
        + [dma] * 23,
        compiler_params=pltpu.CompilerParams(
            collective_id=0, has_side_effects=True, vmem_limit_bytes=60 * 1024 * 1024
        ),
        cost_estimate=pl.CostEstimate(
            flops=8_000_000_000, bytes_accessed=8_000_000, transcendentals=4_000_000
        ),
        name="genomic_forward",
    )(
        codes.reshape(T, PATCH),
        e,
        g1.reshape(1, D),
        w,
        sharp,
        exit_map,
        g2.reshape(1, D),
        widen,
        narrow,
        conv,
    )


def solution(mesh):
    in_specs = (
        P("seq"),
        P(None, "mp"),
        P(),
        P(None, "mp"),
        P("mp"),
        P("mp", None),
        P(),
        P(None, "mp"),
        P("mp", None),
        P(None, None, "mp"),
    )
    return jax.shard_map(
        per_device, mesh=mesh, in_specs=in_specs, out_specs=P("mp", "seq"), check_vma=False
    )
```

time: 467 us -> 146 us (0.31)
  the two profiles are of different devices: /device:TPU:1 before, /device:TPU:0 now
where the time goes in v1:
time: 146 us
  Pallas kernels  134 us (92%)
  local copies, waits for them, and re-layouts  10.9 us (7%)
    pallas_call x1, Pallas kernels, per_device(): pl.pallas_call(kernel, out_shape=jax.ShapeDtypeStruct((OUTS, 2 * T), BF),...  134 us
    unnamed x6, local copies, waits for them, and re-layouts  8.35 us

profile of v1, /device:TPU:0, one launch (start us, length us, event | category | flops | bytes accessed | tf_op | source)
XLA Modules:
  0.0 145.6 jit_solution(8455184466429552101)
XLA Ops:
  0.7 1.3 reshape.10.g1_ref
  1.9 1.3 reshape.11.g2_ref
  3.2 1.8 %copy.11.e_hbm = bf16[512,192]{1,0:T(8,128)(2,1)} copy(bf16[512,192]{0,1:T(8,128)(2,1)} %param.11) | data formatting | bytes 393216 | tf_op args[1]
  5.0 0.0 copy-start
  5.0 2.7 %copy.12.w_hbm = bf16[1536,448]{1,0:T(8,128)(2,1)} copy(bf16[1536,448]{0,1:T(8,128)(2,1)} %param.13) | data formatting | bytes 2752512 | tf_op args[3]
  7.7 0.0 copy-done
  7.7 2.3 %copy.13.conv_hbm = bf16[5,1536,96]{2,1,0:T(8,128)(2,1)} copy(bf16[5,1536,96]{1,2,0:T(8,128)(2,1)S(1)} %copy-done) | data formatting | bytes 2949120 | tf_op args[9]
  10.0 134.0 %genomic_forward.1 = bf16[96,1024]{1,0:T(8,128)(2,1)} custom-call(s32[512,128]{1,0:T(8,128)} %bitcast.1, bf16[512,192]{1,0:T(8,128)(2,1)} %copy.11.e_hbm, bf16[1,1536]{1,0:T(2,128)(2,1)} %reshape.10.g1_ref, bf16[1536,448]{1,0:T(8,128)(2,1)} %copy.12.w_hbm, f32[1]{0:T(128)S(6)} %copy.15.sharp_ref, bf16[192,1536]{1,0:T(8,128)(2,1)} %exit_hbm.1, ...), custom_call_target="tpu_custom_call" | custom-call | flops 8000000000 | bytes 8000000 | tf_op jit(solution)/shard_map/genomic_forward/pallas_call | solution.py:408
  144.0 1.6 %copy.16 = bf16[96,1024]{1,0:T(8,128)(2,1)} copy(bf16[96,1024]{1,0:T(8,128)(2,1)} %genomic_forward.1) | data formatting | bytes 393216
Async XLA Ops:
  5.0 2.7 %copy-start = (bf16[5,1536,96]{1,2,0:T(8,128)(2,1)S(1)}, bf16[5,1536,96]{1,2,0:T(8,128)(2,1)}, u32[]{:S(2)}) copy-start(bf16[5,1536,96]{1,2,0:T(8,128)(2,1)} %param.19) | copy-start | bytes 4423684

commit v2 on v1

v2 whole, which is shorter than its diff:
```python
import jax
import jax.numpy as jnp
from jax import lax
from jax.experimental import pallas as pl
from jax.experimental.pallas import tpu as pltpu
from jax.sharding import PartitionSpec as P

MESH = pl.DeviceIdType.MESH
BF = jnp.bfloat16
F32 = jnp.float32

D = 1536
T = 512
PROBE = 128
VALUE = 192
HIDDEN = 384
OUTS = 96
PATCH = 128
EPS = 1e-06
LOG2E = 1.4426950408889634


def dot(a, b):
    return jnp.dot(a, b, preferred_element_type=F32)


def dot_nt(a, b):
    return lax.dot_general(a, b, (((1,), (1,)), ((), ())), preferred_element_type=F32)


def dot_tn(a, b):
    return lax.dot_general(a, b, (((0,), (0,)), ((), ())), preferred_element_type=F32)


def one_hot_codes(codes):
    wide = codes.astype(F32)
    parts = [jnp.where(wide == float(b), 1.0, 0.0).astype(BF) for b in range(4)]
    return jnp.concatenate(parts, axis=1)


def token_columns(row, width):
    high = row.astype(BF)
    low = (row - high.astype(F32)).astype(BF)
    both = jnp.concatenate(
        [jnp.broadcast_to(high, (16, T)), jnp.broadcast_to(low, (16, T))], axis=0
    )
    return dot_tn(both, jnp.full((32, width), 1.0 / 16.0, BF))


def kernel(
    codes_hbm,
    e_hbm,
    g1_ref,
    w_hbm,
    sharp_ref,
    exit_hbm,
    g2_ref,
    widen_hbm,
    narrow_hbm,
    conv_hbm,
    out_ref,
    codes_i,
    codes_all,
    codes_sib,
    e_loc,
    et_full,
    w_loc,
    wg_t,
    m_t,
    exit_full,
    exit_t,
    stream_t,
    u_all,
    u_sib,
    keys,
    vals,
    queries,
    acc,
    part_recv,
    att_send,
    att_full,
    mixed_t,
    widen_loc,
    widen_t,
    narrow_loc,
    narrow_t,
    inner_t,
    rs_sib_send,
    rs_sib,
    rs_send,
    rs_half,
    rs_recv,
    fin_full,
    conv_loc,
    conv_t,
    edge_send,
    edge_recv,
    out_send,
    out_recv,
    in_sem,
    *sems,
):
    pairs = [sems[2 * i : 2 * i + 2] for i in range(17)]
    codes_sems, za_sems, zb_sems, w_sems, e_sems, ef_sems, x_sems, xf_sems = pairs[:8]
    u_sems, p_sems, att_sems, attf_sems, sib_sems, sum_sems, fin_sems, finf_sems = pairs[8:16]
    edge_sems = pairs[16]

    s = lax.axis_index("seq")
    m = lax.axis_index("mp")
    core = s % 2
    j = s // 2
    z = j % 4
    y_lo = j // 4
    x = m % 4
    hi = m // 4
    sib = s + 1 - 2 * core
    m4 = (m + 4) % 8
    s8 = (s + 8) % 16
    native = core == hi
    shard = core * 4 + x

    def send(src, dst, sems, d, dev):
        return pltpu.make_async_remote_copy(
            src_ref=src,
            dst_ref=dst,
            send_sem=sems[0].at[d],
            recv_sem=sems[1].at[d],
            device_id=dev,
            device_id_type=MESH,
        )

    pending = []

    def push(src, dst, sems, d, dev):
        copy = send(src, dst, sems, d, dev)
        copy.start()
        pending.append(copy)

    def arrive(dst, sems, d):
        send(dst, dst, sems, d, (sib, m)).wait_recv()

    class Ring:
        def __init__(self, piece, sems, right, left, other=None, sib_sems=None):
            self.piece, self.sems, self.right, self.left = piece, sems, right, left
            self.other, self.sib_sems = other, sib_sems

        def go(self, block, half, d, dev):
            push(self.piece(block, half), self.piece(block, half), self.sems, d, dev)

        def forward(self, block, half, d):
            if self.sib_sems is not None:
                push(self.piece(block, half), self.piece(block, half), self.sib_sems, d, (sib, m))

        def start(self):
            self.go(0, 0, 0, self.right)
            self.go(0, 1, 1, self.left)
            self.go(0, 1, 2, self.right)
            self.go(0, 0, 3, self.left)
            self.forward(0, 0, 0)
            self.forward(0, 1, 1)

        def relay(self):
            arrive(self.piece(3, 0), self.sems, 0)
            self.go(3, 0, 4, self.right)
            arrive(self.piece(1, 1), self.sems, 1)
            self.go(1, 1, 5, self.left)
            self.forward(3, 0, 2)
            self.forward(1, 1, 3)

        def near(self):
            arrive(self.piece(3, 1), self.sems, 2)
            self.forward(3, 1, 4)
            arrive(self.piece(1, 0), self.sems, 3)
            self.forward(1, 0, 5)

        def opposite(self):
            arrive(self.piece(2, 0), self.sems, 4)
            self.forward(2, 0, 6)
            arrive(self.piece(2, 1), self.sems, 5)
            self.forward(2, 1, 7)

        def others(self):
            for d, (block, half) in enumerate(
                [(0, 0), (0, 1), (3, 0), (1, 1), (3, 1), (1, 0), (2, 0), (2, 1)]
            ):
                arrive(self.other(block, half), self.sib_sems, d)

    def x_ring(ref, ring_sems, forward_sems):
        def of(c):
            def piece(block, half):
                first = (c * 4 + (x + block) % 4) * 192 + half * 96
                return ref.at[pl.ds(pl.multiple_of(first, 96), 96)]

            return piece

        right = (s, hi * 4 + (x + 1) % 4)
        left = (s, hi * 4 + (x + 3) % 4)
        return Ring(of(core), ring_sems, right, left, of(1 - core), forward_sems)

    def z_ring(y, ring_sems):
        def piece(block, half):
            return codes_all.at[y * 4 + (z + block) % 4, pl.ds(half * 256, 256)]

        right = ((y_lo * 4 + (z + 1) % 4) * 2 + core, m)
        left = ((y_lo * 4 + (z + 3) % 4) * 2 + core, m)
        return Ring(piece, ring_sems, right, left)

    def seq_peer(d):
        return (2 * ((j + d) % 8) + core, m)

    def shard_rows(index):
        return pl.ds(pl.multiple_of(index * 192, 192), 192)

    my_rows = shard_rows(shard)

    codes_in = pltpu.make_async_copy(codes_hbm, codes_i, in_sem.at[0])
    codes_in.start()
    w_in = pltpu.make_async_copy(w_hbm, w_loc, in_sem.at[1])
    weights = [
        (e_hbm, e_loc),
        (exit_hbm, exit_full.at[my_rows]),
        (widen_hbm, widen_loc),
        (narrow_hbm, narrow_loc),
        (conv_hbm, conv_loc),
    ]
    weights_in = [
        pltpu.make_async_copy(src, dst, in_sem.at[2 + i]) for i, (src, dst) in enumerate(weights)
    ]
    weights_out = [send(src, dst, w_sems, i, (s8, m4)) for i, (src, dst) in enumerate(weights)]

    @pl.when(native)
    def _():
        weights_in[0].start()

    w_in.start()

    @pl.when(native)
    def _():
        for copy in weights_in[1:]:
            copy.start()

    def weight_here(i):
        @pl.when(native)
        def _():
            weights_in[i].wait()

        @pl.when(jnp.logical_not(native))
        def _():
            weights_out[i].wait_recv()

    barrier = pltpu.get_barrier_semaphore()
    x_e = x_ring(et_full, e_sems, ef_sems)
    x_exit = x_ring(exit_full, x_sems, xf_sems)
    x_att = x_ring(att_full, att_sems, attf_sems)
    x_fin = x_ring(fin_full, fin_sems, finf_sems)
    z_own = z_ring(y_lo, za_sems)
    z_other = z_ring(1 - y_lo, zb_sems)
    far = (s + 14 + 4 * hi) % 16
    greet = [seq_peer(d) for d in range(1, 8)]
    greet += [x_e.right, x_e.left, (sib, m), (s8, m4), (sib, m4), (s, m4), (far, m4)]
    for dev in greet:
        pl.semaphore_signal(barrier, inc=1, device_id=dev, device_id_type=MESH)

    rows = lax.broadcasted_iota(jnp.int32, (T, T), 0)
    cols = lax.broadcasted_iota(jnp.int32, (T, T), 1)
    order = jnp.where(rows == 4 * (cols % PATCH) + cols // PATCH, 1.0, 0.0).astype(BF)
    codes_in.wait()
    codes_all[j] = codes_i[...].astype(BF)
    pl.semaphore_wait(barrier, len(greet))

    @pl.when(native)
    def _():
        for copy in weights_out[:4]:
            copy.start()

    push(codes_all.at[j], codes_all.at[j], codes_sems, 1, (s8, m))
    z_own.start()
    push(codes_all.at[j], codes_sib, codes_sems, 0, (sib, m))
    weight_here(0)
    et_full[my_rows, :] = dot(e_loc[...], order).astype(BF)
    x_e.start()
    z_own.relay()

    w_in.wait()
    gain = g1_ref[...].astype(F32).reshape(1, D)
    wg_t[0:448, :] = (w_loc[...].astype(F32) * gain).astype(BF)
    wg_t[448:512, :] = jnp.zeros((64, D), BF)

    x_e.relay()
    j_other = (1 - y_lo) * 4 + z
    arrive(codes_all.at[j_other], codes_sems, 1)
    z_other.start()
    x_e.near()
    x_e.opposite()
    weight_here(1)
    x_exit.start()
    x_e.others()

    def stream_of(codes):
        hot = one_hot_codes(codes)

        def step(i, total):
            at = pl.ds(pl.multiple_of(i * 256, 256), 256)
            tile = dot_nt(et_full[at, :], hot).astype(BF)
            stream_t[at, :] = tile
            wide = tile.astype(F32)
            return total + jnp.sum(wide * wide, axis=0, keepdims=True)

        return lax.fori_loop(0, D // 256, step, jnp.zeros((1, T), F32))

    u_all[j] = jnp.broadcast_to(stream_of(codes_all[j]) / D + EPS, (8, T))
    push(u_all.at[j], u_sib, u_sems, 0, (sib, m))
    for d in range(1, 8):
        push(u_all.at[j], u_all.at[j], u_sems, d, seq_peer(d))
    z_other.relay()

    m_t[...] = dot(wg_t[...], et_full[...]).astype(BF)

    lanes = lax.broadcasted_iota(jnp.int32, (T, 256), 1)

    def keys_values(block, at):
        hot = one_hot_codes(codes_all[block])
        raw = dot_nt(hot, m_t[128:512, :])
        spread = token_columns(u_all[block][0:1], 128)
        key = raw[:, :128]
        mean = jnp.mean(key * key, axis=1, keepdims=True)
        keys[at, :] = (key * lax.rsqrt(mean + EPS * spread)).astype(BF)
        inverse = lax.rsqrt(spread)
        value = raw[:, 128:] * jnp.concatenate([inverse, inverse], axis=1)
        vals[at, :] = jnp.where(lanes < VALUE, value, 1.0).astype(BF)

    factor = sharp_ref[0] * (LOG2E / PROBE)

    def make_queries(slot, codes, u_row):
        raw = dot_nt(one_hot_codes(codes), m_t[0:128, :])
        spread = token_columns(u_row, 128)
        mean = jnp.mean(raw * raw, axis=1, keepdims=True)
        queries[slot] = (raw * (lax.rsqrt(mean + EPS * spread) * factor)).astype(BF)

    keys_values(j, pl.ds(0, T))
    make_queries(1, codes_all[j], u_all[j][0:1])
    arrive(codes_sib, codes_sems, 0)
    arrive(u_sib, u_sems, 0)
    make_queries(0, codes_sib[...], u_sib[0:1])

    z_own.near()
    z_own.opposite()
    z_other.near()
    z_other.opposite()
    for d in range(1, 8):
        block = (j + 8 - d) % 8
        arrive(u_all.at[block], u_sems, d)
        keys_values(block, pl.ds(d * T, T))

    def attend(slot):
        def chunk(q, _):
            at = pl.ds(pl.multiple_of(q * 256, 256), 256)
            asked = queries[slot, at, :]

            def step(k, total):
                span = pl.ds(pl.multiple_of(k * 1024, 1024), 1024)
                weights = jnp.exp2(dot_nt(asked, keys[span, :])).astype(BF)
                return total + dot(weights, vals[span, :])

            acc[slot, at, :] = lax.fori_loop(0, 4, step, jnp.zeros((256, 256), F32), unroll=True)
            return 0

        lax.fori_loop(0, 2, chunk, 0)

    def attended():
        whole = acc[1] + part_recv[...]
        return (whole[:, :VALUE] / whole[:, VALUE : VALUE + 1]).astype(BF).T

    part = send(acc.at[0], part_recv, p_sems, 0, (sib, m))
    moved = send(att_send, att_full.at[shard_rows(m)], p_sems, 1, (sib, m4))
    slot = jnp.where(native, 0, 1)
    attend(slot)

    @pl.when(native)
    def _():
        part.start()

    x_exit.relay()

    @pl.when(jnp.logical_not(native))
    def _():
        part.wait_recv()
        att_send[...] = attended()
        moved.start()

    attend(1 - slot)

    @pl.when(native)
    def _():
        part.wait_recv()
        att_full[my_rows, :] = attended()

    @pl.when(jnp.logical_not(native))
    def _():
        part.start()
        moved.wait_recv()

    x_att.start()

    weight_here(2)
    gain = g2_ref[...].astype(F32).reshape(1, D)
    widen_t[...] = (widen_loc[...].T.astype(F32) * gain).astype(BF)
    x_exit.near()
    x_exit.opposite()
    x_att.relay()
    x_exit.others()

    @pl.when(native)
    def _():
        weights_out[4].start()

    @pl.when(jnp.logical_not(native))
    def _():
        stream_of(codes_sib[...])

    def turn_exit(i, _):
        at = pl.ds(pl.multiple_of(i * 256, 256), 256)
        exit_t[at, :] = exit_full[:, at].T
        return 0

    lax.fori_loop(0, D // 256, turn_exit, 0)
    x_att.near()
    x_att.opposite()
    x_att.others()

    def exit_step(i, total):
        at = pl.ds(pl.multiple_of(i * 256, 256), 256)
        tile = (stream_t[at, :].astype(F32) + dot(exit_t[at, :], att_full[...])).astype(BF)
        mixed_t[at, :] = tile
        wide = tile.astype(F32)
        return total + jnp.sum(wide * wide, axis=0, keepdims=True)

    squares = lax.fori_loop(0, D // 256, exit_step, jnp.zeros((1, T), F32))
    second_scale = lax.rsqrt(squares / D + EPS)
    inner = dot(widen_t[...], mixed_t[...]) * second_scale
    inner_t[...] = jnp.maximum(inner, 0.0).astype(BF)

    weight_here(3)
    narrow_t[...] = narrow_loc[...].T

    def partial(c, block):
        return dot(narrow_t[shard_rows(c * 4 + (x + block) % 4), :], inner_t[...])

    for block in (2, 1, 3, 0):
        rs_sib_send[block] = partial(1 - core, block).astype(BF)
        push(rs_sib_send.at[block], rs_sib.at[block], sib_sems, block, (sib, m))

    def pair_sum(block):
        mine = partial(core, block)
        arrive(rs_sib.at[block], sib_sems, block)
        return mine + rs_sib[block].astype(F32)

    rs_send[2] = pair_sum(2).astype(BF)
    push(rs_send.at[2, pl.ds(0, 96)], rs_half.at[0], sum_sems, 0, x_fin.right)
    push(rs_send.at[2, pl.ds(96, 96)], rs_half.at[1], sum_sems, 1, x_fin.left)
    right_sum = pair_sum(1)
    left_sum = pair_sum(3)
    arrive(rs_half.at[0], sum_sems, 0)
    rs_send[1, 0:96] = (right_sum[0:96] + rs_half[0].astype(F32)).astype(BF)
    rs_send[1, 96:192] = right_sum[96:192].astype(BF)
    push(rs_send.at[1], rs_recv.at[0], sum_sems, 2, x_fin.right)
    arrive(rs_half.at[1], sum_sems, 1)
    rs_send[3, 0:96] = left_sum[0:96].astype(BF)
    rs_send[3, 96:192] = (left_sum[96:192] + rs_half[1].astype(F32)).astype(BF)
    push(rs_send.at[3], rs_recv.at[1], sum_sems, 3, x_fin.left)
    total = mixed_t[my_rows, :].astype(F32) + pair_sum(0)
    arrive(rs_recv.at[0], sum_sems, 2)
    arrive(rs_recv.at[1], sum_sems, 3)
    fin_full[my_rows, :] = (total + rs_recv[0].astype(F32) + rs_recv[1].astype(F32)).astype(BF)
    x_fin.start()

    weight_here(4)
    first = conv_loc[0].astype(F32)
    second = conv_loc[1].astype(F32)
    third = conv_loc[2].astype(F32)
    fourth = conv_loc[3].astype(F32)
    last = conv_loc[4].astype(F32)

    def put_tap(index, even, odd):
        conv_t[index, 0:OUTS, :] = even.astype(BF)
        conv_t[index, OUTS : 2 * OUTS, :] = odd.astype(BF)

    put_tap(0, first + second, first)
    put_tap(1, third + fourth, second + third)
    put_tap(2, last, fourth + last)

    x_fin.relay()
    x_fin.near()
    x_fin.opposite()
    x_fin.others()

    edge_send[0] = dot(conv_t[0], fin_full[:, T - 128 :])
    edge_send[1] = dot(conv_t[2], fin_full[:, :128])
    push(edge_send.at[0], edge_recv.at[0], edge_sems, 0, ((s + 2 * hi) % 16, m4))
    push(edge_send.at[1], edge_recv.at[1], edge_sems, 1, ((s + 14 + 2 * hi) % 16, m4))
    before = dot(conv_t[0], fin_full[...])
    here = dot(conv_t[1], fin_full[...])
    after = dot(conv_t[2], fin_full[...])
    arrive(edge_recv.at[0], edge_sems, 0)
    arrive(edge_recv.at[1], edge_sems, 1)
    place = 2 * j + hi
    left = jnp.where(place > 0, edge_recv[0][:, 127:128], 0.0)
    right = jnp.where(place < 15, edge_recv[1][:, 0:1], 0.0)
    before = jnp.concatenate([left, before[:, : T - 1]], axis=1)
    after = jnp.concatenate([after[:, 1:], right], axis=1)
    result = (before + here + after).astype(BF)
    rows = lax.broadcasted_iota(jnp.int32, (256, 256), 0)
    cols = lax.broadcasted_iota(jnp.int32, (256, 256), 1)
    weave = jnp.where(cols == 2 * (rows % 128) + rows // 128, 1.0, 0.0).astype(BF)
    for b in range(4):
        pair = jnp.concatenate(
            [
                result[:OUTS, b * 128 : (b + 1) * 128],
                result[OUTS:, b * 128 : (b + 1) * 128],
            ],
            axis=1,
        )
        out_send[:, b * 256 : (b + 1) * 256] = dot(pair, weave).astype(BF)

    placed = send(out_send, out_recv, edge_sems, 2, (sib, m4))

    @pl.when(native)
    def _():
        out_ref[...] = out_send[...]

    @pl.when(jnp.logical_not(native))
    def _():
        placed.start()
        placed.wait_recv()
        out_ref[...] = out_recv[...]

    part.wait_send()

    @pl.when(native)
    def _():
        for copy in weights_out:
            copy.wait_send()

    @pl.when(jnp.logical_not(native))
    def _():
        moved.wait_send()
        placed.wait_send()

    for copy in pending:
        copy.wait_send()


def per_device(codes, e, g1, w, sharp, exit_map, g2, widen, narrow, conv):
    any_space = pl.BlockSpec(memory_space=pl.ANY)
    vmem = pl.BlockSpec(memory_space=pltpu.VMEM)
    smem = pl.BlockSpec(memory_space=pltpu.SMEM)
    dma = pltpu.SemaphoreType.DMA((8,))
    return pl.pallas_call(
        kernel,
        out_shape=jax.ShapeDtypeStruct((OUTS, 2 * T), BF),
        in_specs=[
            any_space,
            any_space,
            vmem,
            any_space,
            smem,
            any_space,
            vmem,
            any_space,
            any_space,
            any_space,
        ],
        out_specs=vmem,
        scratch_shapes=[
            pltpu.VMEM((T, PATCH), jnp.int32),
            pltpu.VMEM((8, T, PATCH), BF),
            pltpu.VMEM((T, PATCH), BF),
            pltpu.VMEM((192, T), BF),
            pltpu.VMEM((D, T), BF),
            pltpu.VMEM((448, D), BF),
            pltpu.VMEM((T, D), BF),
            pltpu.VMEM((T, T), BF),
            pltpu.VMEM((D, D), BF),
            pltpu.VMEM((D, D), BF),
            pltpu.VMEM((D, T), BF),
            pltpu.VMEM((8, 8, T), F32),
            pltpu.VMEM((8, T), F32),
            pltpu.VMEM((8 * T, PROBE), BF),
            pltpu.VMEM((8 * T, 256), BF),
            pltpu.VMEM((2, T, PROBE), BF),
            pltpu.VMEM((2, T, 256), F32),
            pltpu.VMEM((T, 256), F32),
            pltpu.VMEM((192, T), BF),
            pltpu.VMEM((D, T), BF),
            pltpu.VMEM((D, T), BF),
            pltpu.VMEM((D, HIDDEN), BF),
            pltpu.VMEM((HIDDEN, D), BF),
            pltpu.VMEM((HIDDEN, D), BF),
            pltpu.VMEM((D, HIDDEN), BF),
            pltpu.VMEM((HIDDEN, T), BF),
            pltpu.VMEM((4, 192, T), BF),
            pltpu.VMEM((4, 192, T), BF),
            pltpu.VMEM((4, 192, T), BF),
            pltpu.VMEM((2, 96, T), BF),
            pltpu.VMEM((2, 192, T), BF),
            pltpu.VMEM((D, T), BF),
            pltpu.VMEM((5, OUTS, D), BF),
            pltpu.VMEM((3, 2 * OUTS, D), BF),
            pltpu.VMEM((2, 2 * OUTS, 128), F32),
            pltpu.VMEM((2, 2 * OUTS, 128), F32),
            pltpu.VMEM((OUTS, 2 * T), BF),
            pltpu.VMEM((OUTS, 2 * T), BF),
        ]
        + [dma] * 35,
        compiler_params=pltpu.CompilerParams(
            collective_id=0, has_side_effects=True, vmem_limit_bytes=60 * 1024 * 1024
        ),
        cost_estimate=pl.CostEstimate(
            flops=8_000_000_000, bytes_accessed=8_000_000, transcendentals=4_000_000
        ),
        name="genomic_forward",
    )(
        codes.reshape(T, PATCH),
        e.T,
        g1,
        w.T,
        sharp,
        exit_map,
        g2,
        widen,
        narrow,
        conv.transpose(0, 2, 1),
    )


def solution(mesh):
    in_specs = (
        P("seq"),
        P(None, "mp"),
        P(),
        P(None, "mp"),
        P("mp"),
        P("mp", None),
        P(),
        P(None, "mp"),
        P("mp", None),
        P(None, None, "mp"),
    )
    return jax.shard_map(
        per_device, mesh=mesh, in_specs=in_specs, out_specs=P("mp", "seq"), check_vma=False
    )
```

time: 146 us -> 99.9 us (0.68)
  the two profiles are of different devices: /device:TPU:0 before, /device:TPU:1 now
where the time goes in v2:
time: 99.9 us; the launch traced here: 99.6 us
  Pallas kernels  97.3 us (97%)
  local copies, waits for them, and re-layouts  1.62 us (2%)
    pallas_call x1, Pallas kernels, per_device(): pl.pallas_call(kernel, out_shape=jax.ShapeDtypeStruct((OUTS, 2 * T), BF),...  97.3 us

profile of v2, /device:TPU:1, one launch (start us, length us, event | category | flops | bytes accessed | tf_op | source)
XLA Modules:
  0.0 99.6 jit_solution(15299275755168603824)
XLA Ops:
  0.7 97.3 %genomic_forward.1 = bf16[96,1024]{1,0:T(8,128)(2,1)} custom-call(s32[512,128]{1,0:T(8,128)} %bitcast.6, bf16[192,512]{1,0:T(8,128)(2,1)} %bitcast.7, bf16[1536]{0:T(1024)(128)(2,1)} %g1_ref.1, bf16[448,1536]{1,0:T(8,128)(2,1)} %bitcast.5, f32[1]{0:T(128)S(6)} %copy.12.sharp_ref, bf16[192,1536]{1,0:T(8,128)(2,1)} %exit_hbm.1, bf16[1536]{0:T(1024)(128)(2,1)} %g2_ref.1, ...), custom_call_target="tpu_custom_call" | custom-call | flops 8000000000 | bytes 8000000 | tf_op jit(solution)/shard_map/genomic_forward/pallas_call | solution.py:558
  98.0 1.6 %copy.13 = bf16[96,1024]{1,0:T(8,128)(2,1)} copy(bf16[96,1024]{1,0:T(8,128)(2,1)} %genomic_forward.1) | data formatting | bytes 393216

commit v3 on v2

v3 whole, which is shorter than its diff:
```python
import jax
import jax.numpy as jnp
from jax import lax
from jax.experimental import pallas as pl
from jax.experimental.pallas import tpu as pltpu
from jax.sharding import PartitionSpec as P

MESH = pl.DeviceIdType.MESH
BF = jnp.bfloat16
F32 = jnp.float32

D = 1536
T = 512
TH = 256
PROBE = 128
VALUE = 192
HIDDEN = 384
OUTS = 96
PATCH = 128
EPS = 1e-06
LOG2E = 1.4426950408889634


def dot(a, b):
    return jnp.dot(a, b, preferred_element_type=F32)


def dot_nt(a, b):
    return lax.dot_general(a, b, (((1,), (1,)), ((), ())), preferred_element_type=F32)


def dot_tn(a, b):
    return lax.dot_general(a, b, (((0,), (0,)), ((), ())), preferred_element_type=F32)


def one_hot_codes(codes):
    wide = codes.astype(F32)
    parts = [jnp.where(wide == float(b), 1.0, 0.0).astype(BF) for b in range(4)]
    return jnp.concatenate(parts, axis=1)


def token_columns(row, width):
    high = row.astype(BF)
    low = (row - high.astype(F32)).astype(BF)
    both = jnp.concatenate(
        [jnp.broadcast_to(high, (16, T)), jnp.broadcast_to(low, (16, T))], axis=0
    )
    return dot_tn(both, jnp.full((32, width), 1.0 / 16.0, BF))


def kernel(
    codes_hbm,
    e_hbm,
    g1_ref,
    w_hbm,
    sharp_ref,
    exit_hbm,
    g2_ref,
    widen_hbm,
    narrow_hbm,
    conv_hbm,
    out_ref,
    codes_i,
    codes_all,
    codes_sib,
    e_loc,
    et_full,
    w_loc,
    wg_t,
    m_t,
    exit_full,
    stream,
    u_all,
    u_sib,
    keys,
    vals,
    queries,
    part_send,
    part_recv,
    att_send,
    att_full,
    att,
    mixed,
    widen_all,
    narrow_loc,
    narrow_t,
    rs_send,
    rs_half,
    rs_recv,
    fin_full,
    conv_all,
    conv_t,
    edge_send,
    edge_recv,
    out_send,
    out_recv,
    in_sem,
    *sems,
):
    pairs = [sems[2 * i : 2 * i + 2] for i in range(15)]
    codes_sems, za_sems, zb_sems, w_sems, wf_sems, e_sems, ef_sems, x_sems = pairs[:8]
    xf_sems, u_sems, p_sems, att_sems, sum_sems, fin_sems, edge_sems = pairs[8:]

    s = lax.axis_index("seq")
    m = lax.axis_index("mp")
    core = s % 2
    j = s // 2
    z = j % 4
    y_lo = j // 4
    x = m % 4
    hi = m // 4
    sib = s + 1 - 2 * core
    m4 = (m + 4) % 8
    s8 = (s + 8) % 16

    def send(src, dst, sems, d, dev):
        return pltpu.make_async_remote_copy(
            src_ref=src,
            dst_ref=dst,
            send_sem=sems[0].at[d],
            recv_sem=sems[1].at[d],
            device_id=dev,
            device_id_type=MESH,
        )

    pending = []

    def push(src, dst, sems, d, dev):
        copy = send(src, dst, sems, d, dev)
        copy.start()
        pending.append(copy)

    def arrive(dst, sems, d):
        send(dst, dst, sems, d, (sib, m)).wait_recv()

    class Ring:
        def __init__(self, piece, sems, right, left, other=None, sib_sems=None):
            self.piece, self.sems, self.right, self.left = piece, sems, right, left
            self.other, self.sib_sems = other, sib_sems

        def go(self, block, which, d, dev):
            push(self.piece(block, which), self.piece(block, which), self.sems, d, dev)

        def forward(self, block, which, d):
            if self.sib_sems is not None:
                piece = self.piece(block, which)
                push(piece, piece, self.sib_sems, d, (sib, m))

        def start(self, which):
            if which == 0:
                self.go(0, 0, 0, self.right)
                self.go(0, 0, 3, self.left)
            else:
                self.go(0, 1, 1, self.left)
                self.go(0, 1, 2, self.right)
                self.forward(0, 1, 0)

        def relay(self):
            arrive(self.piece(3, 0), self.sems, 0)
            self.go(3, 0, 4, self.right)
            self.forward(3, 0, 1)
            arrive(self.piece(1, 1), self.sems, 1)
            self.go(1, 1, 5, self.left)
            self.forward(1, 1, 2)

        def near(self):
            arrive(self.piece(1, 0), self.sems, 3)
            self.forward(1, 0, 3)
            arrive(self.piece(3, 1), self.sems, 2)
            self.forward(3, 1, 4)

        def opposite(self):
            arrive(self.piece(2, 0), self.sems, 4)
            self.forward(2, 0, 5)
            arrive(self.piece(2, 1), self.sems, 5)
            self.forward(2, 1, 6)

        def others(self):
            order = [(0, 1), (3, 0), (1, 1), (1, 0), (3, 1), (2, 0), (2, 1)]
            for d, (block, which) in enumerate(order):
                arrive(self.other(block, which), self.sib_sems, d)

    right = (s, hi * 4 + (x + 1) % 4)
    left = (s, hi * 4 + (x + 3) % 4)

    def shard(block, which):
        h = hi if which == 0 else 1 - hi
        return h * 4 + (x + block) % 4

    def shard_rows(block, which):
        return pl.ds(pl.multiple_of(shard(block, which) * 192, 192), 192)

    def whole_ring(ref, ring_sems):
        return Ring(lambda block, which: ref.at[shard_rows(block, which)], ring_sems, right, left)

    def half_ring(ref, ring_sems, sib_sems):
        def of(c):
            def piece(block, which):
                first = shard(block, which) * 192 + c * 96
                return ref.at[pl.ds(pl.multiple_of(first, 96), 96)]

            return piece

        return Ring(of(core), ring_sems, right, left, of(1 - core), sib_sems)

    def z_ring(y, ring_sems):
        def piece(block, which):
            return codes_all.at[y * 4 + (z + block) % 4, pl.ds(which * 256, 256)]

        ahead = ((y_lo * 4 + (z + 1) % 4) * 2 + core, m)
        behind = ((y_lo * 4 + (z + 3) % 4) * 2 + core, m)
        return Ring(piece, ring_sems, ahead, behind)

    def seq_peer(d):
        return (2 * ((j + d) % 8) + core, m)

    my_rows = shard_rows(0, 0)
    own_half = pl.ds(pl.multiple_of(core * 96, 96), 96)
    widen_half = pl.ds(pl.multiple_of(core * 768, 768), 768)
    conv_half = pl.ds(pl.multiple_of(core * 48, 48), 48)
    other_widen_half = pl.ds(pl.multiple_of((1 - core) * 768, 768), 768)
    other_conv_half = pl.ds(pl.multiple_of((1 - core) * 48, 48), 48)

    local = [
        pltpu.make_async_copy(src, dst, in_sem.at[i])
        for i, (src, dst) in enumerate(
            [
                (codes_hbm, codes_i),
                (e_hbm, e_loc),
                (w_hbm, w_loc),
                (exit_hbm, exit_full.at[my_rows]),
                (narrow_hbm, narrow_loc),
                (widen_hbm, widen_all.at[hi]),
                (conv_hbm, conv_all.at[hi]),
            ]
        )
    ]
    for copy in local:
        copy.start()

    x_e = half_ring(et_full, e_sems, ef_sems)
    x_exit = half_ring(exit_full, x_sems, xf_sems)
    x_att = whole_ring(att_full, att_sems)
    x_fin = whole_ring(fin_full, fin_sems)
    z_own = z_ring(y_lo, za_sems)
    z_other = z_ring(1 - y_lo, zb_sems)

    barrier = pltpu.get_barrier_semaphore()
    greet = [(sib, m), right, left, (s8, m4), (s8, m), z_own.right, z_own.left]
    for dev in greet:
        pl.semaphore_signal(barrier, inc=1, device_id=dev, device_id_type=MESH)

    rows = lax.broadcasted_iota(jnp.int32, (T, T), 0)
    cols = lax.broadcasted_iota(jnp.int32, (T, T), 1)
    order = jnp.where(rows == 4 * (cols % PATCH) + cols // PATCH, 1.0, 0.0).astype(BF)
    local[0].wait()
    codes_all[j] = codes_i[...].astype(BF)
    local[1].wait()
    et_full[my_rows, :] = dot(e_loc[...], order).astype(BF)

    local[2].wait()
    gain = g1_ref[...].astype(F32).reshape(1, D)
    wg_t[0:448, :] = (w_loc[...].astype(F32) * gain).astype(BF)
    wg_t[448:512, :] = jnp.zeros((64, D), BF)

    pl.semaphore_wait(barrier, len(greet))

    x_e.start(0)
    push(x_e.piece(0, 0), x_e.piece(0, 0), w_sems, 0, (s8, m4))
    push(codes_all.at[j], codes_all.at[j], codes_sems, 1, (s8, m))
    z_own.start(0)
    z_own.start(1)
    push(codes_all.at[j], codes_sib, codes_sems, 0, (sib, m))
    push(exit_hbm.at[own_half], x_exit.piece(0, 0), w_sems, 1, (s8, m4))
    push(widen_hbm.at[widen_half], widen_all.at[hi, widen_half], w_sems, 2, (s8, m4))

    arrive(x_e.piece(0, 1), w_sems, 0)
    x_e.start(1)
    z_own.relay()
    x_e.relay()
    arrive(codes_all.at[(1 - y_lo) * 4 + z], codes_sems, 1)
    z_other.start(0)
    z_other.start(1)
    local[4].wait()
    narrow_t[hi] = narrow_loc[...].T
    mine = narrow_t.at[hi, widen_half]
    push(mine, mine, w_sems, 3, (s8, m4))
    x_e.near()
    x_e.opposite()
    local[3].wait()
    x_exit.start(0)
    z_other.relay()
    x_e.others()
    arrive(x_exit.piece(0, 1), w_sems, 1)
    x_exit.start(1)

    def stream_step(hot):
        def step(i, total):
            at = pl.ds(pl.multiple_of(i * 256, 256), 256)
            wide = dot_nt(et_full[at, :], hot).astype(BF).astype(F32)
            return total + jnp.sum(wide * wide, axis=0, keepdims=True)

        return step

    squares = lax.fori_loop(
        0, D // 256, stream_step(one_hot_codes(codes_all[j])), jnp.zeros((1, T), F32)
    )
    u_all[j] = jnp.broadcast_to(squares / D + EPS, (8, T))
    push(u_all.at[j], u_sib, u_sems, 0, (sib, m))
    z_own.near()
    z_own.opposite()
    z_other.near()
    z_other.opposite()
    for d in range(1, 8):
        push(u_all.at[j], u_all.at[j], u_sems, d, seq_peer(d))

    m_t[...] = dot(wg_t[...], et_full[...]).astype(BF)

    lanes = lax.broadcasted_iota(jnp.int32, (T, 256), 1)

    def keys_values(block, at):
        hot = one_hot_codes(codes_all[block])
        raw = dot_nt(hot, m_t[128:512, :])
        spread = token_columns(u_all[block][0:1], 128)
        key = raw[:, :128]
        mean = jnp.mean(key * key, axis=1, keepdims=True)
        keys[at, :] = (key * lax.rsqrt(mean + EPS * spread)).astype(BF)
        inverse = lax.rsqrt(spread)
        value = raw[:, 128:] * jnp.concatenate([inverse, inverse], axis=1)
        vals[at, :] = jnp.where(lanes < VALUE, value, 1.0).astype(BF)

    factor = sharp_ref[0] * (LOG2E / PROBE)

    def make_queries(slot, codes, u_row):
        raw = dot_nt(one_hot_codes(codes), m_t[0:128, :])
        spread = token_columns(u_row, 128)
        mean = jnp.mean(raw * raw, axis=1, keepdims=True)
        queries[slot] = (raw * (lax.rsqrt(mean + EPS * spread) * factor)).astype(BF)

    keys_values(j, pl.ds(0, T))
    make_queries(core, codes_all[j], u_all[j][0:1])
    arrive(codes_sib, codes_sems, 0)
    arrive(u_sib, u_sems, 0)
    make_queries(1 - core, codes_sib[...], u_sib[0:1])
    for d in range(1, 8):
        block = (j + 8 - d) % 8
        arrive(u_all.at[block], u_sems, d)
        keys_values(block, pl.ds(d * T, T))

    def attend(slot, half):
        asked = queries[slot, pl.ds(pl.multiple_of(half * TH, TH), TH), :]

        def step(k, total):
            span = pl.ds(pl.multiple_of(k * 1024, 1024), 1024)
            weights = jnp.exp2(dot_nt(asked, keys[span, :])).astype(BF)
            return total + dot(weights, vals[span, :])

        return lax.fori_loop(0, 4, step, jnp.zeros((TH, 256), F32), unroll=True)

    def exchange(slot, which):
        part_send[which] = attend(slot, 1 - core)
        push(part_send.at[which], part_recv.at[which], p_sems, which, (sib, m))

    def attended(slot, which):
        whole = attend(slot, core)
        arrive(part_recv.at[which], p_sems, which)
        whole = whole + part_recv[which]
        return (whole[:, :VALUE] / whole[:, VALUE : VALUE + 1]).astype(BF).T

    exchange(1 - hi, 1)
    att_send[...] = attended(1 - hi, 1)
    push(att_send, att_full.at[my_rows], p_sems, 2, (s, m4))
    x_exit.relay()
    exchange(hi, 0)
    arrive(att_full.at[shard_rows(0, 1)], p_sems, 2)
    x_att.start(1)
    x_exit.near()
    att_full[my_rows, :] = attended(hi, 0)
    x_att.start(0)

    foreign_widen = widen_all.at[1 - hi, widen_half]
    arrive(foreign_widen, w_sems, 2)
    push(foreign_widen, foreign_widen, wf_sems, 0, (sib, m))
    x_exit.opposite()
    x_att.relay()

    def group_stream(codes):
        hot = one_hot_codes(codes)

        def step(i, _):
            at = pl.ds(pl.multiple_of(i * 256, 256), 256)
            stream[:, at] = dot_nt(hot, et_full[at, :]).astype(BF)
            return 0

        lax.fori_loop(0, D // 256, step, 0)

    half_rows = pl.ds(pl.multiple_of(core * TH, TH), TH)

    @pl.when(core == hi)
    def _():
        group_stream(codes_all[j, half_rows])

    @pl.when(core != hi)
    def _():
        group_stream(codes_sib[half_rows, :])

    foreign_narrow = narrow_t.at[1 - hi, widen_half]
    arrive(foreign_narrow, w_sems, 3)
    push(foreign_narrow, foreign_narrow, wf_sems, 1, (sib, m))
    x_exit.others()
    push(
        conv_hbm.at[:, conv_half], conv_all.at[hi, :, conv_half], w_sems, 4, (s8, m4)
    )
    x_att.near()
    x_att.opposite()
    for b in range(4):
        att[:, b * 384 : (b + 1) * 384] = att_full[b * 384 : (b + 1) * 384, :].T

    def exit_step(i, total):
        at = pl.ds(pl.multiple_of(i * 256, 256), 256)
        tile = (stream[:, at].astype(F32) + dot(att[...], exit_full[:, at])).astype(BF)
        mixed[:, at] = tile
        wide = tile.astype(F32)
        return total + jnp.sum(wide * wide, axis=1, keepdims=True)

    squares = lax.fori_loop(0, D // 256, exit_step, jnp.zeros((TH, 1), F32))
    second_scale = lax.rsqrt(squares / D + EPS)
    gain = g2_ref[...].astype(F32).reshape(1, D)
    scaled = (mixed[...].astype(F32) * gain).astype(BF)
    local[5].wait()
    arrive(widen_all.at[1 - hi, other_widen_half], wf_sems, 0)
    inner = [
        jnp.maximum(dot(scaled, widen_all[h]) * second_scale, 0.0).astype(BF) for h in range(2)
    ]

    arrive(narrow_t.at[1 - hi, other_widen_half], wf_sems, 1)

    def partial(block, which):
        at = shard_rows(block, which)
        return dot_nt(narrow_t[0, at, :], inner[0]) + dot_nt(narrow_t[1, at, :], inner[1])

    def give(index, value, dst, d, dev):
        rs_send[index] = value.astype(BF)
        push(rs_send.at[index], dst, sum_sems, d, dev)

    give(0, partial(2, 0), rs_half.at[0], 0, right)
    give(1, partial(2, 1), rs_half.at[1], 1, left)
    give(2, partial(1, 1), rs_recv.at[0, 1], 2, right)
    give(3, partial(3, 0), rs_recv.at[1, 0], 3, left)
    right_sum = partial(1, 0)
    left_sum = partial(3, 1)
    arrive(rs_half.at[0], sum_sems, 0)
    give(4, right_sum + rs_half[0].astype(F32), rs_recv.at[0, 0], 4, right)
    arrive(rs_half.at[1], sum_sems, 1)
    give(5, left_sum + rs_half[1].astype(F32), rs_recv.at[1, 1], 5, left)

    def finish(which, from_left, from_right):
        shifted = lax.broadcasted_iota(jnp.int32, (192, D), 0) + shard(0, which) * 192
        pick = jnp.where(lax.broadcasted_iota(jnp.int32, (192, D), 1) == shifted, 1.0, 0.0)
        total = partial(0, which) + dot_nt(pick.astype(BF), mixed[...])
        arrive(rs_recv.at[0, which], sum_sems, from_left)
        arrive(rs_recv.at[1, which], sum_sems, from_right)
        total = total + rs_recv[0, which].astype(F32) + rs_recv[1, which].astype(F32)
        fin_full[shard_rows(0, which), :] = total.astype(BF)
        x_fin.start(which)

    finish(0, 4, 3)
    finish(1, 2, 5)

    foreign_conv = conv_all.at[1 - hi, :, conv_half]
    arrive(foreign_conv, w_sems, 4)
    push(foreign_conv, foreign_conv, wf_sems, 2, (sib, m))
    x_fin.relay()
    local[6].wait()
    arrive(conv_all.at[1 - hi, :, other_conv_half], wf_sems, 2)
    for h in range(2):
        taps = [conv_all[h, k].astype(F32) for k in range(5)]
        folded = [
            (taps[0] + taps[1], taps[0]),
            (taps[2] + taps[3], taps[1] + taps[2]),
            (taps[4], taps[3] + taps[4]),
        ]
        for index, (even, odd) in enumerate(folded):
            conv_t[index, h * 192 : h * 192 + OUTS, :] = even.astype(BF)
            conv_t[index, h * 192 + OUTS : (h + 1) * 192, :] = odd.astype(BF)

    x_fin.near()
    x_fin.opposite()

    edge_send[0] = dot(conv_t[0], fin_full[:, TH - 128 :]).astype(BF)
    edge_send[1] = dot(conv_t[2], fin_full[:, :128]).astype(BF)
    next_s = (s + 16 + (1 - core) + core * (2 * hi - 1)) % 16
    prev_s = (s + 16 - core + (1 - core) * (2 * hi - 1)) % 16
    push(edge_send.at[0], edge_recv.at[0], edge_sems, 0, (next_s, (m + 4 * core) % 8))
    push(edge_send.at[1], edge_recv.at[1], edge_sems, 1, (prev_s, (m + 4 - 4 * core) % 8))
    place = 4 * j + 2 * hi + core
    rows = lax.broadcasted_iota(jnp.int32, (256, 256), 0)
    cols = lax.broadcasted_iota(jnp.int32, (256, 256), 1)
    weave = jnp.where(cols == 2 * (rows % 128) + rows // 128, 1.0, 0.0).astype(BF)

    def taps_of(which):
        h = hi if which == 0 else 1 - hi
        at = pl.ds(pl.multiple_of(h * 192, 192), 192)
        return at, [dot(conv_t[k, at, :], fin_full[...]) for k in range(3)]

    def outputs(at, products):
        before, here, after = products
        left_edge = jnp.where(place > 0, edge_recv[0, at, :][:, 127:128].astype(F32), 0.0)
        right_edge = jnp.where(place < 31, edge_recv[1, at, :][:, 0:1].astype(F32), 0.0)
        before = jnp.concatenate([left_edge, before[:, : TH - 1]], axis=1)
        after = jnp.concatenate([after[:, 1:], right_edge], axis=1)
        result = (before + here + after).astype(BF)
        woven = []
        for b in range(2):
            span = slice(b * 128, (b + 1) * 128)
            both = jnp.concatenate([result[:OUTS, span], result[OUTS:, span]], axis=1)
            woven.append(dot(both, weave).astype(BF))
        return jnp.concatenate(woven, axis=1)

    foreign = taps_of(1)
    arrive(edge_recv.at[0], edge_sems, 0)
    arrive(edge_recv.at[1], edge_sems, 1)
    out_send[1] = outputs(*foreign)
    push(out_send.at[1], out_recv.at[core], edge_sems, 4 + core, (2 * j + hi, m4))
    mine = outputs(*taps_of(0))
    out_send[0] = mine
    to_sibling = send(out_send.at[0], out_recv.at[core], edge_sems, 2 + core, (sib, m))

    @pl.when(core == hi)
    def _():
        out_ref[:, pl.ds(pl.multiple_of(core * T, T), T)] = mine
        arrive(out_recv.at[1 - core], edge_sems, 3 - core)
        out_ref[:, pl.ds(pl.multiple_of((1 - core) * T, T), T)] = out_recv[1 - core]

    @pl.when(core != hi)
    def _():
        to_sibling.start()
        arrive(out_recv.at[0], edge_sems, 4)
        arrive(out_recv.at[1], edge_sems, 5)
        out_ref[:, :T] = out_recv[0]
        out_ref[:, T:] = out_recv[1]
        to_sibling.wait_send()

    for copy in pending:
        copy.wait_send()


def per_device(codes, e, g1, w, sharp, exit_map, g2, widen, narrow, conv):
    any_space = pl.BlockSpec(memory_space=pl.ANY)
    vmem = pl.BlockSpec(memory_space=pltpu.VMEM)
    smem = pl.BlockSpec(memory_space=pltpu.SMEM)
    dma = pltpu.SemaphoreType.DMA((8,))
    return pl.pallas_call(
        kernel,
        out_shape=jax.ShapeDtypeStruct((OUTS, 2 * T), BF),
        in_specs=[
            any_space,
            any_space,
            vmem,
            any_space,
            smem,
            any_space,
            vmem,
            any_space,
            any_space,
            any_space,
        ],
        out_specs=vmem,
        scratch_shapes=[
            pltpu.VMEM((T, PATCH), jnp.int32),
            pltpu.VMEM((8, T, PATCH), BF),
            pltpu.VMEM((T, PATCH), BF),
            pltpu.VMEM((192, T), BF),
            pltpu.VMEM((D, T), BF),
            pltpu.VMEM((448, D), BF),
            pltpu.VMEM((T, D), BF),
            pltpu.VMEM((T, T), BF),
            pltpu.VMEM((D, D), BF),
            pltpu.VMEM((TH, D), BF),
            pltpu.VMEM((8, 8, T), F32),
            pltpu.VMEM((8, T), F32),
            pltpu.VMEM((8 * T, PROBE), BF),
            pltpu.VMEM((8 * T, 256), BF),
            pltpu.VMEM((2, T, PROBE), BF),
            pltpu.VMEM((2, TH, 256), F32),
            pltpu.VMEM((2, TH, 256), F32),
            pltpu.VMEM((192, TH), BF),
            pltpu.VMEM((D, TH), BF),
            pltpu.VMEM((TH, D), BF),
            pltpu.VMEM((TH, D), BF),
            pltpu.VMEM((2, D, HIDDEN), BF),
            pltpu.VMEM((HIDDEN, D), BF),
            pltpu.VMEM((2, D, HIDDEN), BF),
            pltpu.VMEM((6, 192, TH), BF),
            pltpu.VMEM((2, 192, TH), BF),
            pltpu.VMEM((2, 2, 192, TH), BF),
            pltpu.VMEM((D, TH), BF),
            pltpu.VMEM((2, 5, OUTS, D), BF),
            pltpu.VMEM((3, 4 * OUTS, D), BF),
            pltpu.VMEM((2, 4 * OUTS, 128), BF),
            pltpu.VMEM((2, 4 * OUTS, 128), BF),
            pltpu.VMEM((2, OUTS, T), BF),
            pltpu.VMEM((2, OUTS, T), BF),
        ]
        + [dma] * 31,
        compiler_params=pltpu.CompilerParams(
            collective_id=0, has_side_effects=True, vmem_limit_bytes=60 * 1024 * 1024
        ),
        cost_estimate=pl.CostEstimate(
            flops=8_000_000_000, bytes_accessed=8_000_000, transcendentals=4_000_000
        ),
        name="genomic_forward",
    )(
        codes.reshape(T, PATCH),
        e.T,
        g1,
        w.T,
        sharp,
        exit_map,
        g2,
        widen,
        narrow,
        conv.transpose(0, 2, 1),
    )


def solution(mesh):
    in_specs = (
        P("seq"),
        P(None, "mp"),
        P(),
        P(None, "mp"),
        P("mp"),
        P("mp", None),
        P(),
        P(None, "mp"),
        P("mp", None),
        P(None, None, "mp"),
    )
    return jax.shard_map(
        per_device, mesh=mesh, in_specs=in_specs, out_specs=P("mp", "seq"), check_vma=False
    )
```

time: 99.9 us -> 90.6 us (0.907)
  Pallas kernels: 97.3 us -> 87.3 us
    pallas_call x1, Pallas kernels: 97.3 us -> 87.3 us  [per_device(): pl.pallas_call(kernel, out_shape=jax.ShapeDtypeStruct((OUTS, 2 * T), BF),...]
where the time goes in v3:
time: 90.6 us; the launch traced here: 89.6 us
  Pallas kernels  87.3 us (96%)
  local copies, waits for them, and re-layouts  1.62 us (2%)
    pallas_call x1, Pallas kernels, per_device(): pl.pallas_call(kernel, out_shape=jax.ShapeDtypeStruct((OUTS, 2 * T), BF),...  87.3 us

profile of v3, /device:TPU:1, one launch (start us, length us, event | category | flops | bytes accessed | tf_op | source)
XLA Modules:
  0.0 89.6 jit_solution(8164581986719049549)
XLA Ops:
  0.7 87.3 %genomic_forward.1 = bf16[96,1024]{1,0:T(8,128)(2,1)} custom-call(s32[512,128]{1,0:T(8,128)} %bitcast.6, bf16[192,512]{1,0:T(8,128)(2,1)} %bitcast.7, bf16[1536]{0:T(1024)(128)(2,1)} %g1_ref.1, bf16[448,1536]{1,0:T(8,128)(2,1)} %bitcast.5, f32[1]{0:T(128)S(6)} %copy.12.sharp_ref, bf16[192,1536]{1,0:T(8,128)(2,1)} %exit_hbm.1, bf16[1536]{0:T(1024)(128)(2,1)} %g2_ref.1, ...), custom_call_target="tpu_custom_call" | custom-call | flops 8000000000 | bytes 8000000 | tf_op jit(solution)/shard_map/genomic_forward/pallas_call | solution.py:553
  87.9 1.6 %copy.13 = bf16[96,1024]{1,0:T(8,128)(2,1)} copy(bf16[96,1024]{1,0:T(8,128)(2,1)} %genomic_forward.1) | data formatting | bytes 393216

commit v4 on v3

--- a/solution.py
+++ b/solution.py
@@ -70,6 +70,7 @@
     m_t,
     exit_full,
     stream,
+    sq_all,
     u_all,
     u_sib,
     keys,
@@ -81,25 +82,29 @@
     att_full,
     att,
     mixed,
+    mixed_t,
     widen_all,
     narrow_loc,
     narrow_t,
+    inner_t,
     rs_send,
     rs_half,
     rs_recv,
     fin_full,
     conv_all,
     conv_t,
-    edge_send,
-    edge_recv,
+    halo_send,
+    halo_recv,
+    edges,
     out_send,
     out_recv,
     in_sem,
     *sems,
 ):
     pairs = [sems[2 * i : 2 * i + 2] for i in range(15)]
-    codes_sems, za_sems, zb_sems, w_sems, wf_sems, e_sems, ef_sems, x_sems = pairs[:8]
-    xf_sems, u_sems, p_sems, att_sems, sum_sems, fin_sems, edge_sems = pairs[8:]
+    codes_sems, w_sems, wf_sems, e_sems, ef_sems, x_sems = pairs[:6]
+    xf_sems, u_sems, p_sems, att_sems, sum_sems, fin_sems, edge_sems, sq_sems = pairs[6:14]
+    out_sems = pairs[14]
 
     s = lax.axis_index("seq")
     m = lax.axis_index("mp")
@@ -155,13 +160,15 @@
                 self.go(0, 1, 2, self.right)
                 self.forward(0, 1, 0)
 
-        def relay(self):
-            arrive(self.piece(3, 0), self.sems, 0)
-            self.go(3, 0, 4, self.right)
-            self.forward(3, 0, 1)
-            arrive(self.piece(1, 1), self.sems, 1)
-            self.go(1, 1, 5, self.left)
-            self.forward(1, 1, 2)
+        def relay(self, which):
+            if which == 0:
+                arrive(self.piece(3, 0), self.sems, 0)
+                self.go(3, 0, 4, self.right)
+                self.forward(3, 0, 1)
+            else:
+                arrive(self.piece(1, 1), self.sems, 1)
+                self.go(1, 1, 5, self.left)
+                self.forward(1, 1, 2)
 
         def near(self):
             arrive(self.piece(1, 0), self.sems, 3)
@@ -180,6 +187,25 @@
             for d, (block, which) in enumerate(order):
                 arrive(self.other(block, which), self.sib_sems, d)
 
+    class Direct(Ring):
+        def start(self, which):
+            across = (s, hi * 4 + (x + 2) % 4)
+            for k, dev in enumerate((self.right, self.left, across)):
+                self.go(0, which, 3 * which + k, dev)
+            if which == 1:
+                self.forward(0, 1, 0)
+
+        def land(self, which):
+            for k, block in enumerate((3, 1, 2)):
+                arrive(self.piece(block, which), self.sems, 3 * which + k)
+                self.forward(block, which, 1 + 3 * which + k)
+
+        def others(self):
+            arrive(self.other(0, 1), self.sib_sems, 0)
+            for which in range(2):
+                for k, block in enumerate((3, 1, 2)):
+                    arrive(self.other(block, which), self.sib_sems, 1 + 3 * which + k)
+
     right = (s, hi * 4 + (x + 1) % 4)
     left = (s, hi * 4 + (x + 3) % 4)
 
@@ -193,7 +219,7 @@
     def whole_ring(ref, ring_sems):
         return Ring(lambda block, which: ref.at[shard_rows(block, which)], ring_sems, right, left)
 
-    def half_ring(ref, ring_sems, sib_sems):
+    def half_ring(kind, ref, ring_sems, sib_sems):
         def of(c):
             def piece(block, which):
                 first = shard(block, which) * 192 + c * 96
@@ -201,15 +227,7 @@
 
             return piece
 
-        return Ring(of(core), ring_sems, right, left, of(1 - core), sib_sems)
-
-    def z_ring(y, ring_sems):
-        def piece(block, which):
-            return codes_all.at[y * 4 + (z + block) % 4, pl.ds(which * 256, 256)]
-
-        ahead = ((y_lo * 4 + (z + 1) % 4) * 2 + core, m)
-        behind = ((y_lo * 4 + (z + 3) % 4) * 2 + core, m)
-        return Ring(piece, ring_sems, ahead, behind)
+        return kind(of(core), ring_sems, right, left, of(1 - core), sib_sems)
 
     def seq_peer(d):
         return (2 * ((j + d) % 8) + core, m)
@@ -238,15 +256,15 @@
     for copy in local:
         copy.start()
 
-    x_e = half_ring(et_full, e_sems, ef_sems)
-    x_exit = half_ring(exit_full, x_sems, xf_sems)
+    x_e = half_ring(Direct, et_full, e_sems, ef_sems)
+    x_exit = half_ring(Ring, exit_full, x_sems, xf_sems)
     x_att = whole_ring(att_full, att_sems)
     x_fin = whole_ring(fin_full, fin_sems)
-    z_own = z_ring(y_lo, za_sems)
-    z_other = z_ring(1 - y_lo, zb_sems)
 
     barrier = pltpu.get_barrier_semaphore()
-    greet = [(sib, m), right, left, (s8, m4), (s8, m), z_own.right, z_own.left]
+    greet = [(sib, m), (s8, m4)]
+    greet += [(s, (m + d) % 8) for d in range(1, 8)]
+    greet += [seq_peer(d) for d in range(1, 8)]
     for dev in greet:
         pl.semaphore_signal(barrier, inc=1, device_id=dev, device_id_type=MESH)
 
@@ -263,57 +281,41 @@
     wg_t[0:448, :] = (w_loc[...].astype(F32) * gain).astype(BF)
     wg_t[448:512, :] = jnp.zeros((64, D), BF)
 
+    shard_stream = dot_nt(et_full[my_rows, :], one_hot_codes(codes_all[j])).astype(BF).astype(F32)
+    squares = jnp.sum(shard_stream * shard_stream, axis=0, keepdims=True)
+    sq_all[0] = squares
+
     pl.semaphore_wait(barrier, len(greet))
 
+    for d in range(1, 8):
+        push(sq_all.at[0], sq_all.at[d], sq_sems, d, (s, (m + d) % 8))
     x_e.start(0)
     push(x_e.piece(0, 0), x_e.piece(0, 0), w_sems, 0, (s8, m4))
-    push(codes_all.at[j], codes_all.at[j], codes_sems, 1, (s8, m))
-    z_own.start(0)
-    z_own.start(1)
+    for d in (4, 1, 7, 5, 3, 2, 6):
+        push(codes_all.at[j], codes_all.at[j], codes_sems, d, seq_peer(d))
     push(codes_all.at[j], codes_sib, codes_sems, 0, (sib, m))
     push(exit_hbm.at[own_half], x_exit.piece(0, 0), w_sems, 1, (s8, m4))
     push(widen_hbm.at[widen_half], widen_all.at[hi, widen_half], w_sems, 2, (s8, m4))
 
+    local[4].wait()
+    narrow_t[hi] = narrow_loc[...].T
     arrive(x_e.piece(0, 1), w_sems, 0)
     x_e.start(1)
-    z_own.relay()
-    x_e.relay()
-    arrive(codes_all.at[(1 - y_lo) * 4 + z], codes_sems, 1)
-    z_other.start(0)
-    z_other.start(1)
-    local[4].wait()
-    narrow_t[hi] = narrow_loc[...].T
-    mine = narrow_t.at[hi, widen_half]
-    push(mine, mine, w_sems, 3, (s8, m4))
-    x_e.near()
-    x_e.opposite()
     local[3].wait()
     x_exit.start(0)
-    z_other.relay()
+    for d in range(1, 8):
+        arrive(sq_all.at[d], sq_sems, d)
+        squares = squares + sq_all[d]
+    u_all[j] = squares / D + EPS
+    push(u_all.at[j], u_sib, u_sems, 0, (sib, m))
+    for d in range(1, 8):
+        push(u_all.at[j], u_all.at[j], u_sems, d, seq_peer(d))
+    x_e.land(0)
+    x_e.land(1)
     x_e.others()
     arrive(x_exit.piece(0, 1), w_sems, 1)
     x_exit.start(1)
 
-    def stream_step(hot):
-        def step(i, total):
-            at = pl.ds(pl.multiple_of(i * 256, 256), 256)
-            wide = dot_nt(et_full[at, :], hot).astype(BF).astype(F32)
-            return total + jnp.sum(wide * wide, axis=0, keepdims=True)
-
-        return step
-
-    squares = lax.fori_loop(
-        0, D // 256, stream_step(one_hot_codes(codes_all[j])), jnp.zeros((1, T), F32)
-    )
-    u_all[j] = jnp.broadcast_to(squares / D + EPS, (8, T))
-    push(u_all.at[j], u_sib, u_sems, 0, (sib, m))
-    z_own.near()
-    z_own.opposite()
-    z_other.near()
-    z_other.opposite()
-    for d in range(1, 8):
-        push(u_all.at[j], u_all.at[j], u_sems, d, seq_peer(d))
-
     m_t[...] = dot(wg_t[...], et_full[...]).astype(BF)
 
     lanes = lax.broadcasted_iota(jnp.int32, (T, 256), 1)
@@ -321,7 +323,7 @@
     def keys_values(block, at):
         hot = one_hot_codes(codes_all[block])
         raw = dot_nt(hot, m_t[128:512, :])
-        spread = token_columns(u_all[block][0:1], 128)
+        spread = token_columns(u_all[block], 128)
         key = raw[:, :128]
         mean = jnp.mean(key * key, axis=1, keepdims=True)
         keys[at, :] = (key * lax.rsqrt(mean + EPS * spread)).astype(BF)
@@ -338,24 +340,20 @@
         queries[slot] = (raw * (lax.rsqrt(mean + EPS * spread) * factor)).astype(BF)
 
     keys_values(j, pl.ds(0, T))
-    make_queries(core, codes_all[j], u_all[j][0:1])
+    make_queries(core, codes_all[j], u_all[j])
     arrive(codes_sib, codes_sems, 0)
     arrive(u_sib, u_sems, 0)
-    make_queries(1 - core, codes_sib[...], u_sib[0:1])
-    for d in range(1, 8):
+    make_queries(1 - core, codes_sib[...], u_sib[...])
+    for d in (4, 1, 7, 5, 3, 2, 6):
         block = (j + 8 - d) % 8
+        arrive(codes_all.at[block], codes_sems, d)
         arrive(u_all.at[block], u_sems, d)
         keys_values(block, pl.ds(d * T, T))
 
     def attend(slot, half):
         asked = queries[slot, pl.ds(pl.multiple_of(half * TH, TH), TH), :]
-
-        def step(k, total):
-            span = pl.ds(pl.multiple_of(k * 1024, 1024), 1024)
-            weights = jnp.exp2(dot_nt(asked, keys[span, :])).astype(BF)
-            return total + dot(weights, vals[span, :])
-
-        return lax.fori_loop(0, 4, step, jnp.zeros((TH, 256), F32), unroll=True)
+        weights = jnp.exp2(dot_nt(asked, keys[...])).astype(BF)
+        return dot(weights, vals[...])
 
     def exchange(slot, which):
         part_send[which] = attend(slot, 1 - core)
@@ -367,22 +365,24 @@
         whole = whole + part_recv[which]
         return (whole[:, :VALUE] / whole[:, VALUE : VALUE + 1]).astype(BF).T
 
+    x_exit.relay(0)
     exchange(1 - hi, 1)
     att_send[...] = attended(1 - hi, 1)
     push(att_send, att_full.at[my_rows], p_sems, 2, (s, m4))
-    x_exit.relay()
+    narrow_mine = narrow_t.at[hi, widen_half]
+    push(narrow_mine, narrow_mine, w_sems, 3, (s8, m4))
+    push(conv_hbm.at[:, conv_half], conv_all.at[hi, :, conv_half], w_sems, 4, (s8, m4))
     exchange(hi, 0)
+    x_exit.relay(1)
+    att_full[my_rows, :] = attended(hi, 0)
+    x_att.start(0)
     arrive(att_full.at[shard_rows(0, 1)], p_sems, 2)
     x_att.start(1)
-    x_exit.near()
-    att_full[my_rows, :] = attended(hi, 0)
-    x_att.start(0)
 
     foreign_widen = widen_all.at[1 - hi, widen_half]
     arrive(foreign_widen, w_sems, 2)
     push(foreign_widen, foreign_widen, wf_sems, 0, (sib, m))
-    x_exit.opposite()
-    x_att.relay()
+    x_att.relay(0)
 
     def group_stream(codes):
         hot = one_hot_codes(codes)
@@ -404,13 +404,10 @@
     def _():
         group_stream(codes_sib[half_rows, :])
 
-    foreign_narrow = narrow_t.at[1 - hi, widen_half]
-    arrive(foreign_narrow, w_sems, 3)
-    push(foreign_narrow, foreign_narrow, wf_sems, 1, (sib, m))
+    x_att.relay(1)
+    x_exit.near()
+    x_exit.opposite()
     x_exit.others()
-    push(
-        conv_hbm.at[:, conv_half], conv_all.at[hi, :, conv_half], w_sems, 4, (s8, m4)
-    )
     x_att.near()
     x_att.opposite()
     for b in range(4):
@@ -429,15 +426,20 @@
     scaled = (mixed[...].astype(F32) * gain).astype(BF)
     local[5].wait()
     arrive(widen_all.at[1 - hi, other_widen_half], wf_sems, 0)
-    inner = [
-        jnp.maximum(dot(scaled, widen_all[h]) * second_scale, 0.0).astype(BF) for h in range(2)
-    ]
-
+    for h in range(2):
+        inner = jnp.maximum(dot(scaled, widen_all[h]) * second_scale, 0.0).astype(BF)
+        inner_t[h * HIDDEN : (h + 1) * HIDDEN, :] = inner.T
+
+    foreign_narrow = narrow_t.at[1 - hi, widen_half]
+    arrive(foreign_narrow, w_sems, 3)
+    push(foreign_narrow, foreign_narrow, wf_sems, 1, (sib, m))
     arrive(narrow_t.at[1 - hi, other_widen_half], wf_sems, 1)
 
     def partial(block, which):
         at = shard_rows(block, which)
-        return dot_nt(narrow_t[0, at, :], inner[0]) + dot_nt(narrow_t[1, at, :], inner[1])
+        return dot(narrow_t[0, at, :], inner_t[:HIDDEN, :]) + dot(
+            narrow_t[1, at, :], inner_t[HIDDEN:, :]
+        )
 
     def give(index, value, dst, d, dev):
         rs_send[index] = value.astype(BF)
@@ -449,28 +451,48 @@
     give(3, partial(3, 0), rs_recv.at[1, 0], 3, left)
     right_sum = partial(1, 0)
     left_sum = partial(3, 1)
+    mixed_t[...] = mixed[...].T
+    own = [
+        partial(0, which) + mixed_t[shard_rows(0, which), :].astype(F32) for which in range(2)
+    ]
     arrive(rs_half.at[0], sum_sems, 0)
     give(4, right_sum + rs_half[0].astype(F32), rs_recv.at[0, 0], 4, right)
     arrive(rs_half.at[1], sum_sems, 1)
     give(5, left_sum + rs_half[1].astype(F32), rs_recv.at[1, 1], 5, left)
 
     def finish(which, from_left, from_right):
-        shifted = lax.broadcasted_iota(jnp.int32, (192, D), 0) + shard(0, which) * 192
-        pick = jnp.where(lax.broadcasted_iota(jnp.int32, (192, D), 1) == shifted, 1.0, 0.0)
-        total = partial(0, which) + dot_nt(pick.astype(BF), mixed[...])
         arrive(rs_recv.at[0, which], sum_sems, from_left)
         arrive(rs_recv.at[1, which], sum_sems, from_right)
-        total = total + rs_recv[0, which].astype(F32) + rs_recv[1, which].astype(F32)
+        total = own[which] + rs_recv[0, which].astype(F32) + rs_recv[1, which].astype(F32)
         fin_full[shard_rows(0, which), :] = total.astype(BF)
         x_fin.start(which)
 
     finish(0, 4, 3)
     finish(1, 2, 5)
+
+    next_s = (s + 16 + (1 - core) + core * (2 * hi - 1)) % 16
+    prev_s = (s + 16 - core + (1 - core) * (2 * hi - 1)) % 16
+    ends = [
+        fin_full[pl.ds(pl.multiple_of((h * 4 + x) * 192, 192), 192), :] for h in range(2)
+    ]
+    halo_send[0] = jnp.concatenate([end[:, TH - 128 :].T[112:128] for end in ends], axis=1)
+    halo_send[1] = jnp.concatenate([end[:, :128].T[0:16] for end in ends], axis=1)
+    sides = [(next_s, (hi + core) % 2), (prev_s, (hi + 1 - core) % 2)]
+    for side, (to_s, to_hi) in enumerate(sides):
+        for k in range(4):
+            push(
+                halo_send.at[side],
+                halo_recv.at[side * 4 + x],
+                edge_sems,
+                side * 4 + k,
+                (to_s, to_hi * 4 + (x + k) % 4),
+            )
 
     foreign_conv = conv_all.at[1 - hi, :, conv_half]
     arrive(foreign_conv, w_sems, 4)
     push(foreign_conv, foreign_conv, wf_sems, 2, (sib, m))
-    x_fin.relay()
+    x_fin.relay(0)
+    x_fin.relay(1)
     local[6].wait()
     arrive(conv_all.at[1 - hi, :, other_conv_half], wf_sems, 2)
     for h in range(2):
@@ -484,15 +506,24 @@
             conv_t[index, h * 192 : h * 192 + OUTS, :] = even.astype(BF)
             conv_t[index, h * 192 + OUTS : (h + 1) * 192, :] = odd.astype(BF)
 
+    for side in range(2):
+        for k in range(4):
+            arrive(halo_recv.at[side * 4 + (x + 4 - k) % 4], edge_sems, side * 4 + k)
+        row = jnp.concatenate(
+            [
+                halo_recv[side * 4 + chip][:, h * 192 : (h + 1) * 192]
+                for h in range(2)
+                for chip in range(4)
+            ],
+            axis=1,
+        )
+        added = dot_nt(row, conv_t[2 * side]).T
+        column = added[:, 15:16] if side == 0 else added[:, 0:1]
+        edges[side] = jnp.broadcast_to(column, (4 * OUTS, 128))
+
     x_fin.near()
     x_fin.opposite()
 
-    edge_send[0] = dot(conv_t[0], fin_full[:, TH - 128 :]).astype(BF)
-    edge_send[1] = dot(conv_t[2], fin_full[:, :128]).astype(BF)
-    next_s = (s + 16 + (1 - core) + core * (2 * hi - 1)) % 16
-    prev_s = (s + 16 - core + (1 - core) * (2 * hi - 1)) % 16
-    push(edge_send.at[0], edge_recv.at[0], edge_sems, 0, (next_s, (m + 4 * core) % 8))
-    push(edge_send.at[1], edge_recv.at[1], edge_sems, 1, (prev_s, (m + 4 - 4 * core) % 8))
     place = 4 * j + 2 * hi + core
     rows = lax.broadcasted_iota(jnp.int32, (256, 256), 0)
     cols = lax.broadcasted_iota(jnp.int32, (256, 256), 1)
@@ -505,8 +536,8 @@
 
     def outputs(at, products):
         before, here, after = products
-        left_edge = jnp.where(place > 0, edge_recv[0, at, :][:, 127:128].astype(F32), 0.0)
-        right_edge = jnp.where(place < 31, edge_recv[1, at, :][:, 0:1].astype(F32), 0.0)
+        left_edge = jnp.where(place > 0, edges[0, at, :][:, 0:1], 0.0)
+        right_edge = jnp.where(place < 31, edges[1, at, :][:, 0:1], 0.0)
         before = jnp.concatenate([left_edge, before[:, : TH - 1]], axis=1)
         after = jnp.concatenate([after[:, 1:], right_edge], axis=1)
         result = (before + here + after).astype(BF)
@@ -517,26 +548,23 @@
             woven.append(dot(both, weave).astype(BF))
         return jnp.concatenate(woven, axis=1)
 
-    foreign = taps_of(1)
-    arrive(edge_recv.at[0], edge_sems, 0)
-    arrive(edge_recv.at[1], edge_sems, 1)
-    out_send[1] = outputs(*foreign)
-    push(out_send.at[1], out_recv.at[core], edge_sems, 4 + core, (2 * j + hi, m4))
+    out_send[1] = outputs(*taps_of(1))
+    push(out_send.at[1], out_recv.at[core], out_sems, 4 + core, (2 * j + hi, m4))
     mine = outputs(*taps_of(0))
     out_send[0] = mine
-    to_sibling = send(out_send.at[0], out_recv.at[core], edge_sems, 2 + core, (sib, m))
+    to_sibling = send(out_send.at[0], out_recv.at[core], out_sems, 2 + core, (sib, m))
 
     @pl.when(core == hi)
     def _():
         out_ref[:, pl.ds(pl.multiple_of(core * T, T), T)] = mine
-        arrive(out_recv.at[1 - core], edge_sems, 3 - core)
+        arrive(out_recv.at[1 - core], out_sems, 3 - core)
         out_ref[:, pl.ds(pl.multiple_of((1 - core) * T, T), T)] = out_recv[1 - core]
 
     @pl.when(core != hi)
     def _():
         to_sibling.start()
-        arrive(out_recv.at[0], edge_sems, 4)
-        arrive(out_recv.at[1], edge_sems, 5)
+        arrive(out_recv.at[0], out_sems, 4)
+        arrive(out_recv.at[1], out_sems, 5)
         out_ref[:, :T] = out_recv[0]
         out_ref[:, T:] = out_recv[1]
         to_sibling.wait_send()
@@ -577,8 +605,9 @@
             pltpu.VMEM((T, T), BF),
             pltpu.VMEM((D, D), BF),
             pltpu.VMEM((TH, D), BF),
-            pltpu.VMEM((8, 8, T), F32),
-            pltpu.VMEM((8, T), F32),
+            pltpu.VMEM((8, 1, T), F32),
+            pltpu.VMEM((8, 1, T), F32),
+            pltpu.VMEM((1, T), F32),
             pltpu.VMEM((8 * T, PROBE), BF),
             pltpu.VMEM((8 * T, 256), BF),
             pltpu.VMEM((2, T, PROBE), BF),
@@ -588,17 +617,20 @@
             pltpu.VMEM((D, TH), BF),
             pltpu.VMEM((TH, D), BF),
             pltpu.VMEM((TH, D), BF),
+            pltpu.VMEM((D, TH), BF),
             pltpu.VMEM((2, D, HIDDEN), BF),
             pltpu.VMEM((HIDDEN, D), BF),
             pltpu.VMEM((2, D, HIDDEN), BF),
+            pltpu.VMEM((2 * HIDDEN, TH), BF),
             pltpu.VMEM((6, 192, TH), BF),
             pltpu.VMEM((2, 192, TH), BF),
             pltpu.VMEM((2, 2, 192, TH), BF),
             pltpu.VMEM((D, TH), BF),
             pltpu.VMEM((2, 5, OUTS, D), BF),
             pltpu.VMEM((3, 4 * OUTS, D), BF),
-            pltpu.VMEM((2, 4 * OUTS, 128), BF),
-            pltpu.VMEM((2, 4 * OUTS, 128), BF),
+            pltpu.VMEM((2, 16, 2 * 192), BF),
+            pltpu.VMEM((8, 16, 2 * 192), BF),
+            pltpu.VMEM((2, 4 * OUTS, 128), F32),
             pltpu.VMEM((2, OUTS, T), BF),
             pltpu.VMEM((2, OUTS, T), BF),
         ]

time: 90.6 us -> 87.8 us (0.969)
  Pallas kernels: 87.3 us -> 85.4 us
    pallas_call x1, Pallas kernels: 87.3 us -> 85.4 us  [per_device(): pl.pallas_call(kernel, out_shape=jax.ShapeDtypeStruct((OUTS, 2 * T), BF),...]
where the time goes in v4:
time: 87.8 us; the launch traced here: 87.7 us
  Pallas kernels  85.4 us (97%)
  local copies, waits for them, and re-layouts  1.62 us (2%)
    pallas_call x1, Pallas kernels, per_device(): pl.pallas_call(kernel, out_shape=jax.ShapeDtypeStruct((OUTS, 2 * T), BF),...  85.4 us

profile of v4, /device:TPU:1, one launch (start us, length us, event | category | flops | bytes accessed | tf_op | source)
XLA Modules:
  0.0 87.7 jit_solution(15838189601628057393)
XLA Ops:
  0.7 85.4 %genomic_forward.1 = bf16[96,1024]{1,0:T(8,128)(2,1)} custom-call(s32[512,128]{1,0:T(8,128)} %bitcast.6, bf16[192,512]{1,0:T(8,128)(2,1)} %bitcast.7, bf16[1536]{0:T(1024)(128)(2,1)} %g1_ref.1, bf16[448,1536]{1,0:T(8,128)(2,1)} %bitcast.5, f32[1]{0:T(128)S(6)} %copy.12.sharp_ref, bf16[192,1536]{1,0:T(8,128)(2,1)} %exit_hbm.1, bf16[1536]{0:T(1024)(128)(2,1)} %g2_ref.1, ...), custom_call_target="tpu_custom_call" | custom-call | flops 8000000000 | bytes 8000000 | tf_op jit(solution)/shard_map/genomic_forward/pallas_call | solution.py:581
  86.0 1.6 %copy.13 = bf16[96,1024]{1,0:T(8,128)(2,1)} copy(bf16[96,1024]{1,0:T(8,128)(2,1)} %genomic_forward.1) | data formatting | bytes 393216

commit v5 on v4

--- a/solution.py
+++ b/solution.py
@@ -374,10 +374,11 @@
     push(conv_hbm.at[:, conv_half], conv_all.at[hi, :, conv_half], w_sems, 4, (s8, m4))
     exchange(hi, 0)
     x_exit.relay(1)
-    att_full[my_rows, :] = attended(hi, 0)
-    x_att.start(0)
+    own_attended = attended(hi, 0)
     arrive(att_full.at[shard_rows(0, 1)], p_sems, 2)
     x_att.start(1)
+    att_full[my_rows, :] = own_attended
+    x_att.start(0)
 
     foreign_widen = widen_all.at[1 - hi, widen_half]
     arrive(foreign_widen, w_sems, 2)

time: 87.8 us -> 85.8 us (0.977)
  Pallas kernels: 85.4 us -> 83.3 us
    pallas_call x1, Pallas kernels: 85.4 us -> 83.3 us  [per_device(): pl.pallas_call(kernel, out_shape=jax.ShapeDtypeStruct((OUTS, 2 * T), BF),...]
where the time goes in v5:
time: 85.8 us; the launch traced here: 85.6 us
  Pallas kernels  83.3 us (97%)
  local copies, waits for them, and re-layouts  1.62 us (2%)
    pallas_call x1, Pallas kernels, per_device(): pl.pallas_call(kernel, out_shape=jax.ShapeDtypeStruct((OUTS, 2 * T), BF),...  83.3 us

profile of v5, /device:TPU:1, one launch (start us, length us, event | category | flops | bytes accessed | tf_op | source)
XLA Modules:
  0.0 85.6 jit_solution(16487036906319732919)
XLA Ops:
  0.7 83.3 %genomic_forward.1 = bf16[96,1024]{1,0:T(8,128)(2,1)} custom-call(s32[512,128]{1,0:T(8,128)} %bitcast.6, bf16[192,512]{1,0:T(8,128)(2,1)} %bitcast.7, bf16[1536]{0:T(1024)(128)(2,1)} %g1_ref.1, bf16[448,1536]{1,0:T(8,128)(2,1)} %bitcast.5, f32[1]{0:T(128)S(6)} %copy.12.sharp_ref, bf16[192,1536]{1,0:T(8,128)(2,1)} %exit_hbm.1, bf16[1536]{0:T(1024)(128)(2,1)} %g2_ref.1, ...), custom_call_target="tpu_custom_call" | custom-call | flops 8000000000 | bytes 8000000 | tf_op jit(solution)/shard_map/genomic_forward/pallas_call | solution.py:582
  84.0 1.6 %copy.13 = bf16[96,1024]{1,0:T(8,128)(2,1)} copy(bf16[96,1024]{1,0:T(8,128)(2,1)} %genomic_forward.1) | data formatting | bytes 393216

commit v6 on v5

--- a/solution.py
+++ b/solution.py
@@ -187,25 +187,6 @@
             for d, (block, which) in enumerate(order):
                 arrive(self.other(block, which), self.sib_sems, d)
 
-    class Direct(Ring):
-        def start(self, which):
-            across = (s, hi * 4 + (x + 2) % 4)
-            for k, dev in enumerate((self.right, self.left, across)):
-                self.go(0, which, 3 * which + k, dev)
-            if which == 1:
-                self.forward(0, 1, 0)
-
-        def land(self, which):
-            for k, block in enumerate((3, 1, 2)):
-                arrive(self.piece(block, which), self.sems, 3 * which + k)
-                self.forward(block, which, 1 + 3 * which + k)
-
-        def others(self):
-            arrive(self.other(0, 1), self.sib_sems, 0)
-            for which in range(2):
-                for k, block in enumerate((3, 1, 2)):
-                    arrive(self.other(block, which), self.sib_sems, 1 + 3 * which + k)
-
     right = (s, hi * 4 + (x + 1) % 4)
     left = (s, hi * 4 + (x + 3) % 4)
 
@@ -256,7 +237,7 @@
     for copy in local:
         copy.start()
 
-    x_e = half_ring(Direct, et_full, e_sems, ef_sems)
+    x_e = half_ring(Ring, et_full, e_sems, ef_sems)
     x_exit = half_ring(Ring, exit_full, x_sems, xf_sems)
     x_att = whole_ring(att_full, att_sems)
     x_fin = whole_ring(fin_full, fin_sems)
@@ -301,6 +282,8 @@
     narrow_t[hi] = narrow_loc[...].T
     arrive(x_e.piece(0, 1), w_sems, 0)
     x_e.start(1)
+    x_e.relay(0)
+    x_e.relay(1)
     local[3].wait()
     x_exit.start(0)
     for d in range(1, 8):
@@ -310,8 +293,8 @@
     push(u_all.at[j], u_sib, u_sems, 0, (sib, m))
     for d in range(1, 8):
         push(u_all.at[j], u_all.at[j], u_sems, d, seq_peer(d))
-    x_e.land(0)
-    x_e.land(1)
+    x_e.near()
+    x_e.opposite()
     x_e.others()
     arrive(x_exit.piece(0, 1), w_sems, 1)
     x_exit.start(1)

time: 85.8 us -> 87.1 us (1.015)
  Pallas kernels: 83.3 us -> 84.6 us
    pallas_call x1, Pallas kernels: 83.3 us -> 84.6 us  [per_device(): pl.pallas_call(kernel, out_shape=jax.ShapeDtypeStruct((OUTS, 2 * T), BF),...]
where the time goes in v6:
time: 87.1 us; the launch traced here: 86.9 us
  Pallas kernels  84.6 us (97%)
  local copies, waits for them, and re-layouts  1.62 us (2%)
    pallas_call x1, Pallas kernels, per_device(): pl.pallas_call(kernel, out_shape=jax.ShapeDtypeStruct((OUTS, 2 * T), BF),...  84.6 us

profile of v6, /device:TPU:1, one launch (start us, length us, event | category | flops | bytes accessed | tf_op | source)
XLA Modules:
  0.0 86.9 jit_solution(7658040413503694831)
XLA Ops:
  0.7 84.6 %genomic_forward.1 = bf16[96,1024]{1,0:T(8,128)(2,1)} custom-call(s32[512,128]{1,0:T(8,128)} %bitcast.6, bf16[192,512]{1,0:T(8,128)(2,1)} %bitcast.7, bf16[1536]{0:T(1024)(128)(2,1)} %g1_ref.1, bf16[448,1536]{1,0:T(8,128)(2,1)} %bitcast.5, f32[1]{0:T(128)S(6)} %copy.12.sharp_ref, bf16[192,1536]{1,0:T(8,128)(2,1)} %exit_hbm.1, bf16[1536]{0:T(1024)(128)(2,1)} %g2_ref.1, ...), custom_call_target="tpu_custom_call" | custom-call | flops 8000000000 | bytes 8000000 | tf_op jit(solution)/shard_map/genomic_forward/pallas_call | solution.py:565
  85.3 1.6 %copy.13 = bf16[96,1024]{1,0:T(8,128)(2,1)} copy(bf16[96,1024]{1,0:T(8,128)(2,1)} %genomic_forward.1) | data formatting | bytes 393216
